TPU v7x, 32 devices: a whole 2x2x4 slice. The times are simulated.
32 devices in a mesh: gx: 4 (over y, core), gy: 8 (over z, x).
Axes of the slice: x: 2, y: 2, z: 4, core: 2. Of those that a mesh axis runs over, the one named last changes fastest.
Arguments:
- tiles: float32 [2, 3, 16384, 128], P(None, None, ('gx', 'gy')), may hold values from -6 to 6
- tile_owner: int32 [16384, 1], P(('gx', 'gy')), may hold values from 0 to 31; in each aligned block of 512 rows (0 to 511, 512 to 1023, ...) at most 32 rows name the same one
- tile_slot: int32 [16384], P(('gx', 'gy')), may hold values from 0 to 1023
- tile_count: int32 [32], P(('gx', 'gy')), may hold values from 384 to 512, as said below
- green: float32 [2, 6, 1, 2048, 2048], P(None, None, None, ('gx', 'gy')), may hold values from -6 to 6
Outputs:
- field_hat: float32 [2, 3, 1, 2048, 2048], P(None, None, None, ('gx', 'gy'))
Inputs may be any that keep to these rules, and one draw needn't show every extreme that they name: `tile_owner`: within the 512 entries of one device, live or not, no owner is named by more than 32; that many is reached. `tile_count`: some device has all 512 entries live.
All inputs are finite; a program needn't handle non-finite values.
Results may differ from a plain program's by a relative error of at most 0.00007.
Values sent between devices are 32-bit elements; how exact they have to be, the bound alone decides.
No kernel may reach another device: no remote copies, remote signals or barrier semaphores. Data moves between devices by JAX's collectives and lax.ppermute only.
A program may use at most 128 MiB of HBM per device.

v0:
```python
import functools
import math

import jax
import jax.numpy as jnp
import ml_dtypes
import numpy as np
from jax import lax
from jax.experimental import pallas as pl
from jax.experimental.pallas import tpu as pltpu
from jax.sharding import PartitionSpec as P

pair_index = ((0, 3, 4), (3, 1, 5), (4, 5, 2))
by_rows = (((1,), (1,)), ((), ()))


def params(mebibytes):
    return pltpu.CompilerParams(vmem_limit_bytes=mebibytes * 1024 * 1024)


def cost(flops, moved):
    return pl.CostEstimate(flops=flops, bytes_accessed=moved, transcendentals=0)


def angles(rows, columns, length):
    products = np.outer(np.arange(rows), np.arange(columns)) % length
    return 2.0 * math.pi / length * products


def halves(table):
    wide = np.asarray(table, np.float32)
    high = wide.astype(ml_dtypes.bfloat16)
    low = (wide - high.astype(np.float32)).astype(ml_dtypes.bfloat16)
    return jnp.asarray(high), jnp.asarray(low)


def split_two(data):
    high = data.astype(jnp.bfloat16)
    return high, (data - high.astype(jnp.float32)).astype(jnp.bfloat16)


def split_three(data):
    high = data.astype(jnp.bfloat16)
    rest = data - high.astype(jnp.float32)
    middle = rest.astype(jnp.bfloat16)
    return high, middle, (rest - middle.astype(jnp.float32)).astype(jnp.bfloat16)


def dot_rows(left, right):
    return lax.dot_general(left, right, by_rows, preferred_element_type=jnp.float32)


def dot_rows_split(table, data):
    rows, depth = table.shape
    table_high, table_low = split_two(table)
    high, low = split_two(data)
    if depth > 128:
        both = dot_rows(jnp.concatenate([table_high, table_low]), high)
        return both[:rows] + both[rows:] + dot_rows(table_high, low)
    left = jnp.concatenate(
        [
            jnp.concatenate([table_high, table_high], axis=1),
            jnp.concatenate([table_low, jnp.zeros_like(table_low)], axis=1),
        ]
    )
    both = dot_rows(left, jnp.concatenate([high, low], axis=1))
    return both[:rows] + both[rows:]


def flat_fft(values, times):
    length = len(values)
    if length == 1:
        return values
    even = flat_fft(values[0::2], times)
    odd = flat_fft(values[1::2], times)
    lower, upper = [], []
    for k in range(length // 2):
        turned = times(odd[k], k, length)
        lower.append(jax.tree.map(lambda a, b: a + b, even[k], turned))
        upper.append(jax.tree.map(lambda a, b: a - b, even[k], turned))
    return lower + upper


def times_pair(value, k, length):
    real, imag = value
    if k == 0:
        return value
    if 4 * k == length:
        return (imag, -real)
    cos_k = math.cos(2.0 * math.pi * k / length)
    sin_k = math.sin(2.0 * math.pi * k / length)
    return (real * cos_k + imag * sin_k, imag * cos_k - real * sin_k)


def pack_kernel(devices, per_owner, count, me, owner_row, slot_row, tiles, *out):
    listed = owner_row.shape[1]
    comps = tiles.shape[1]
    live_count = count[0]
    owners = owner_row[...]
    live = lax.broadcasted_iota(jnp.int32, (1, listed), 1) < live_count
    place = jnp.where(live, owners ^ me[0], -1)
    named = jnp.where(
        lax.broadcasted_iota(jnp.int32, (devices, listed), 0) == place, 1.0, 0.0
    )
    sender = lax.broadcasted_iota(jnp.int32, (listed, listed), 0)
    reader = lax.broadcasted_iota(jnp.int32, (listed, listed), 1)
    before = jnp.where(sender < reader, 1.0, 0.0).astype(jnp.bfloat16)
    counted = jnp.dot(named.astype(jnp.bfloat16), before, preferred_element_type=jnp.float32)
    rank = jnp.sum(counted * named, axis=0, keepdims=True).astype(jnp.int32)
    target = jnp.where(live, place * per_owner + rank, -1)
    places = lax.broadcasted_iota(jnp.int32, (devices * per_owner, listed), 0)
    chosen = jnp.where(places == target, 1.0, 0.0).astype(jnp.bfloat16)
    for comp in range(comps):
        parts = [part for r in range(2) for part in split_three(tiles[r, comp])]
        got = jnp.dot(
            chosen, jnp.concatenate(parts, axis=1), preferred_element_type=jnp.float32
        )
        for r in range(2):
            one = got[:, 384 * r : 384 * r + 384]
            whole = (one[:, :128] + one[:, 128:256]) + one[:, 256:]
            start = (2 * comp + r) * per_owner
            for part in range(devices):
                out[part][start : start + per_owner, :] = whole[part * per_owner :][:per_owner]
    stated = slot_row[...] + 1
    lane = rank + (place & (128 // per_owner - 1)) * per_owner
    lane_at = lax.broadcasted_iota(jnp.int32, (128, listed), 0)
    ranked = jnp.where(lane_at == lane, 1.0, 0.0).astype(jnp.bfloat16)
    coarse = (named * (stated >> 5).astype(jnp.float32)).astype(jnp.bfloat16)
    fine = (named * (stated & 31).astype(jnp.float32)).astype(jnp.bfloat16)
    slots = 32.0 * dot_rows(coarse, ranked) + dot_rows(fine, ranked)
    for part in range(devices):
        out[part][2 * comps * per_owner :, :] = jnp.broadcast_to(slots[part : part + 1], (8, 128))


def pack(tiles, owner_row, slot_row, count, me, devices, per_owner):
    comps, listed = tiles.shape[1:3]
    rows = 2 * comps * per_owner + 8
    return pl.pallas_call(
        functools.partial(pack_kernel, devices, per_owner),
        out_shape=[jax.ShapeDtypeStruct((rows, 128), jnp.float32)] * devices,
        in_specs=[pl.BlockSpec(memory_space=pltpu.SMEM)] * 2
        + [pl.BlockSpec(memory_space=pltpu.VMEM)] * 3,
        out_specs=[pl.BlockSpec(memory_space=pltpu.VMEM)] * devices,
        compiler_params=params(24),
        cost_estimate=cost(
            devices * per_owner * listed * 768 * 2 * comps, devices * rows * 1024
        ),
    )(count, me, owner_row, slot_row, tiles)


def slab_kernel(comps, x_local, blocks, per_owner, me, table, twist, *refs):
    devices, kept = table.shape[:2]
    data, out = refs[:devices], refs[devices : 2 * devices]
    slab, turned, ordered = refs[2 * devices :]
    entries = devices * per_owner
    y_local = kept * blocks
    wide = 2 * x_local
    shift = blocks.bit_length() - 1
    every = 128 // per_owner
    slots = []
    for start in range(0, devices, every):
        slots.append(sum([one[one.shape[0] - 8 :, :][:1] for one in data[start : start + every]]))
    slot = jnp.concatenate(slots, axis=1).astype(jnp.int32) - 1
    landing = jnp.where(slot >= 0, (slot & (blocks - 1)) * x_local + (slot >> shift), -1)
    for place in range(devices):
        ordered[place * kept : (place + 1) * kept, :] = table[me[0] ^ place]
    for index, comp in enumerate(comps):
        parts = []
        for r in range(2):
            start = (2 * comp + r) * per_owner
            arrived = jnp.concatenate([one[start : start + per_owner, :] for one in data])
            parts.extend(split_two(arrived))
        parts = jnp.concatenate(parts, axis=1)
        for start in range(0, blocks * x_local, 256):
            place = start + lax.broadcasted_iota(jnp.int32, (256, entries), 0)
            chosen = jnp.where(place == landing, 1.0, 0.0).astype(jnp.bfloat16)
            got = jnp.dot(chosen, parts, preferred_element_type=jnp.float32)
            for r in range(2):
                slab[r, start : start + 256, :] = (
                    got[:, 256 * r : 256 * r + 128] + got[:, 256 * r + 128 : 256 * r + 256]
                )

        @pl.loop(0, x_local // 8)
        def _(step):
            at = pl.multiple_of(step * 8, 8)
            values = [
                tuple(slab[r, pl.ds(t * x_local + at, 8), :] for r in range(2))
                for t in range(blocks)
            ]
            waves = flat_fft(values, times_pair)
            for k in range(blocks):
                real, imag = waves[k]
                cos_k, sin_k = twist[0, k : k + 1, :], twist[1, k : k + 1, :]
                new_real = real * cos_k + imag * sin_k
                new_imag = imag * cos_k - real * sin_k
                first = pl.ds(k * wide + at, 8)
                second = pl.ds(k * wide + x_local + at, 8)
                turned[first, :128] = new_real
                turned[first, 128:] = new_imag
                turned[second, :128] = new_imag
                turned[second, 128:] = -new_real

        together = 4
        for start in range(0, blocks, together):
            moved = dot_rows_split(
                ordered[...], turned[start * wide : (start + together) * wide, :]
            )
            for k in range(start, start + together):
                one = moved[:, (k - start) * wide : (k - start + 1) * wide]
                for part in range(devices):
                    rows = pl.ds(index * y_local + k, kept, stride=blocks)
                    out[part][rows, :] = one[part * kept : (part + 1) * kept]


def slab_waves(me, comps, data, x_local, blocks, per_owner):
    devices = len(data)
    y_cells = blocks * 128
    fine = angles(128, 128, 128)
    table = np.concatenate([np.cos(fine), np.sin(fine)], axis=1).astype(np.float32)
    table = table.reshape(devices, 128 // devices, 256)
    twist_angle = angles(blocks, 128, y_cells)
    twist = np.stack([np.cos(twist_angle), np.sin(twist_angle)]).astype(np.float32)
    entries = devices * per_owner
    made = jax.ShapeDtypeStruct((len(comps) * y_cells // devices, 2 * x_local), jnp.float32)
    return pl.pallas_call(
        functools.partial(slab_kernel, comps, x_local, blocks, per_owner),
        out_shape=[made] * devices,
        in_specs=[pl.BlockSpec(memory_space=pltpu.SMEM)]
        + [pl.BlockSpec(memory_space=pltpu.VMEM)] * (2 + devices),
        out_specs=[pl.BlockSpec(memory_space=pltpu.VMEM)] * devices,
        scratch_shapes=[
            pltpu.VMEM((2, blocks * x_local, 128), jnp.float32),
            pltpu.VMEM((blocks * 2 * x_local, 256), jnp.float32),
            pltpu.VMEM((128, 256), jnp.float32),
        ],
        compiler_params=params(24),
        cost_estimate=cost(
            len(comps) * (blocks * x_local * entries * 1024 + y_cells * x_local * 3072),
            len(comps) * (entries * 1024 + y_cells * x_local * 8),
        ),
    )(me, jnp.asarray(table), jnp.asarray(twist), *data)


def swap_parts(value, x_local):
    if 2 * x_local == 128:
        return pltpu.roll(value, x_local, 1)
    return jnp.concatenate([value[:, x_local:], value[:, :x_local]], axis=1)


def x_steps(
    devices, x_local, y_local, index, me, twist, table, data, placed, turned, columns, store
):
    wide = 2 * x_local
    lane = lax.broadcasted_iota(jnp.int32, (1, wide), 1)
    sign = jnp.where(lane < x_local, 1.0, -1.0)
    for place in range(devices):
        placed[me[0] ^ place] = data[place][index * y_local : (index + 1) * y_local, :]

    def times(value, k, length):
        if k == 0:
            return value
        swapped = swap_parts(value, x_local) * sign
        if 4 * k == length:
            return swapped
        cos_k = math.cos(2.0 * math.pi * k / length)
        sin_k = math.sin(2.0 * math.pi * k / length)
        return value * cos_k + swapped * sin_k

    @pl.loop(0, y_local // 8)
    def _(step):
        at = pl.multiple_of(step * 8, 8)
        values = [placed[o, pl.ds(at, 8), :] for o in range(devices)]
        waves = flat_fft(values, times)
        for k in range(devices):
            swapped = swap_parts(waves[k], x_local)
            new = waves[k] * twist[0, k : k + 1, :] + swapped * twist[1, k : k + 1, :]
            turned[k, pl.ds(at, 8), :] = new
            turned[k, pl.ds(y_local + at, 8), :] = swap_parts(new, x_local) * sign

    together = 4
    for start in range(0, devices, together):
        stacked = turned[start : start + together].reshape(together * 2 * y_local, wide)
        moved = dot_rows_split(table[...], stacked)
        for k in range(start, start + together):
            columns[pl.ds(k, x_local, stride=devices), :] = moved[
                :, (k - start) * 2 * y_local : (k - start + 1) * 2 * y_local
            ]
    for start in range(0, devices * x_local, 128):
        store(start, columns[start : start + 128, :].T)


def x_kernel(devices, x_local, y_local, index, me, twist, table, *refs):
    data, out, scratch = refs[:devices], refs[devices], refs[devices + 1 :]

    def store(start, block):
        out[0, :, start : start + 128] = block[:y_local]
        out[1, :, start : start + 128] = block[y_local:]

    x_steps(devices, x_local, y_local, index, me, twist, table, data, *scratch, store)


def last_kernel(devices, x_local, y_local, index, me, twist, table, *refs):
    data, (green, first, second, out) = refs[:devices], refs[devices : devices + 4]
    scratch, (tensor, kept, made, in_sems, out_sems) = refs[devices + 4 :][:3], refs[devices + 7 :]
    x_cells = devices * x_local
    pieces = made.shape[0]
    width = x_cells // pieces
    fetches = [
        pltpu.make_async_copy(first, kept.at[0], in_sems.at[0]),
        pltpu.make_async_copy(second, kept.at[1], in_sems.at[1]),
        pltpu.make_async_copy(green, tensor, in_sems.at[2]),
    ]
    for fetch in fetches:
        fetch.start()

    def store(start, block):
        kept[2, 0, :, start : start + 128] = block[:y_local]
        kept[2, 1, :, start : start + 128] = block[y_local:]

    x_steps(devices, x_local, y_local, index, me, twist, table, data, *scratch, store)
    for fetch in fetches:
        fetch.wait()
    sends = []
    for piece in range(pieces):

        @pl.loop(0, y_local // 8)
        def _(step):
            rows = pl.ds(pl.multiple_of(step * 8, 8), 8)
            columns = pl.ds(piece * width, width)
            waves = [(kept[c, 0, rows, columns], kept[c, 1, rows, columns]) for c in range(3)]
            sums = [[None, None] for _ in range(3)]
            for entry in range(6):
                green_real = tensor[0, entry, rows, columns]
                green_imag = tensor[1, entry, rows, columns]
                for row in range(3):
                    for col in range(3):
                        if pair_index[row][col] != entry:
                            continue
                        real, imag = waves[col]
                        real_term = green_real * real - green_imag * imag
                        imag_term = green_real * imag + green_imag * real
                        old = sums[row]
                        sums[row] = [
                            real_term if old[0] is None else old[0] + real_term,
                            imag_term if old[1] is None else old[1] + imag_term,
                        ]
            for row in range(3):
                made[piece, 0, row, rows, :] = sums[row][0]
                made[piece, 1, row, rows, :] = sums[row][1]

        send = pltpu.make_async_copy(
            made.at[piece],
            out.at[:, :, :, pl.ds(piece * width, width)],
            out_sems.at[piece],
        )
        send.start()
        sends.append(send)
    for send in sends:
        send.wait()


def x_tables(devices, x_local, y_cells):
    x_cells = devices * x_local
    fine = angles(x_local, x_local, x_local)
    scale = 1.0 / math.sqrt(x_cells * y_cells)
    table = np.concatenate([np.cos(fine), np.sin(fine)], axis=1) * scale
    angle = angles(devices, x_local, x_cells)
    cos_a, sin_a = np.cos(angle), np.sin(angle)
    twist = np.stack(
        [np.concatenate([cos_a, cos_a], axis=1), np.concatenate([sin_a, -sin_a], axis=1)]
    )
    return jnp.asarray(twist.astype(np.float32)), jnp.asarray(table.astype(np.float32))


def x_scratch(devices, x_local, y_local):
    return [
        pltpu.VMEM((devices, y_local, 2 * x_local), jnp.float32),
        pltpu.VMEM((devices, 2 * y_local, 2 * x_local), jnp.float32),
        pltpu.VMEM((devices * x_local, 2 * y_local), jnp.float32),
    ]


def x_waves(me, index, data, devices, x_local, y_local, y_cells):
    x_cells = devices * x_local
    return pl.pallas_call(
        functools.partial(x_kernel, devices, x_local, y_local, index),
        out_shape=jax.ShapeDtypeStruct((2, y_local, x_cells), jnp.float32),
        in_specs=[pl.BlockSpec(memory_space=pltpu.SMEM)]
        + [pl.BlockSpec(memory_space=pltpu.VMEM)] * (2 + devices),
        out_specs=pl.BlockSpec(memory_space=pltpu.VMEM),
        scratch_shapes=x_scratch(devices, x_local, y_local),
        compiler_params=params(24),
        cost_estimate=cost(x_cells * y_local * x_local * 24, x_cells * y_local * 16),
    )(me, *x_tables(devices, x_local, y_cells), *data)


def last_waves(me, index, data, green, first, second, devices, x_local, y_local, y_cells):
    x_cells = devices * x_local
    pieces = 8
    return pl.pallas_call(
        functools.partial(last_kernel, devices, x_local, y_local, index),
        out_shape=jax.ShapeDtypeStruct((2, 3, y_local, x_cells), jnp.float32),
        in_specs=[pl.BlockSpec(memory_space=pltpu.SMEM)]
        + [pl.BlockSpec(memory_space=pltpu.VMEM)] * (2 + devices)
        + [pl.BlockSpec(memory_space=pl.ANY)] * 3,
        out_specs=pl.BlockSpec(memory_space=pl.ANY),
        scratch_shapes=x_scratch(devices, x_local, y_local)
        + [
            pltpu.VMEM((2, 6, y_local, x_cells), jnp.float32),
            pltpu.VMEM((3, 2, y_local, x_cells), jnp.float32),
            pltpu.VMEM((pieces, 2, 3, y_local, x_cells // pieces), jnp.float32),
            pltpu.SemaphoreType.DMA((3,)),
            pltpu.SemaphoreType.DMA((pieces,)),
        ],
        compiler_params=params(40),
        cost_estimate=cost(x_cells * y_local * (x_local * 24 + 72), x_cells * y_local * 96),
    )(me, *x_tables(devices, x_local, y_cells), *data, green, first, second)


def exchange(blocks):
    devices = len(blocks)
    far = [m for m in range(devices) if m & 4]
    near = [m for m in range(1, devices) if not m & 4]
    arrived = [blocks[0]] + [None] * (devices - 1)
    for pair in zip(far, near + [None]):
        for m in pair:
            if m is not None:
                moves = [(d, d ^ m) for d in range(devices)]
                arrived[m] = lax.ppermute(blocks[m], ("gx", "gy"), moves)
    return arrived


def per_device(tiles, tile_owner, tile_slot, tile_count, green):
    devices = lax.axis_size("gx") * lax.axis_size("gy")
    tile_total, tile_len = tiles.shape[2], tiles.shape[3]
    planes, y_local, x_cells = green.shape[2:]
    y_cells = y_local * devices
    x_local = x_cells // devices
    blocks = y_cells // tile_len
    per_owner = max(2, 2 * tile_total // devices)
    assert planes == 1 and tile_len == 128
    me = (lax.axis_index("gx") * lax.axis_size("gy") + lax.axis_index("gy")).reshape(1)
    me = me.astype(jnp.int32)
    owner_row, slot_row = tile_owner.reshape(1, tile_total), tile_slot.reshape(1, tile_total)
    green = green.reshape(2, 6, y_local, x_cells)
    arrived = exchange(pack(tiles, owner_row, slot_row, tile_count, me, devices, per_owner))
    moved = {}
    for comps in ((0,), (1, 2)):
        got = exchange(slab_waves(me, comps, arrived, x_local, blocks, per_owner))
        moved.update({comp: (me, i, got) for i, comp in enumerate(comps)})
    sizes = (devices, x_local, y_local, y_cells)
    waves = [x_waves(*moved[comp], *sizes) for comp in range(2)]
    mixed = last_waves(*moved[2], green, *waves, *sizes)
    return mixed.reshape(2, 3, planes, y_local, x_cells)


def solution(mesh):
    in_specs = (
        P(None, None, ("gx", "gy"), None),
        P(("gx", "gy"), None),
        P(("gx", "gy")),
        P(("gx", "gy")),
        P(None, None, None, ("gx", "gy"), None),
    )
    out_specs = P(None, None, None, ("gx", "gy"), None)
    return jax.shard_map(
        per_device, mesh=mesh, in_specs=in_specs, out_specs=out_specs, check_vma=False
    )
```

profile of v0, /device:TPU:0, one launch (start us, length us, event | category | flops | bytes accessed | tf_op | source)
XLA Modules:
  0.0 236.7 jit_solution(5801020180258648262)
XLA Ops:
  3.4 2.9 %shard_map.145 = (f32[200,128]{1,0:T(8,128)S(1)}, f32[200,128]{1,0:T(8,128)S(1)}, f32[200,128]{1,0:T(8,128)S(1)}, f32[200,128]{1,0:T(8,128)S(1)}, f32[200,128]{1...) custom-call(s32[1]{0:T(128)S(6)} %copy.17.count, ...), custom_call_target="tpu_custom_call" | custom-call | flops 2415919104 | bytes 6553600 | tf_op jit(solution)/shard_map/pallas_call | solution.py:138
  6.3 3.0 %collective-permute-start = (f32[200,128]{1,0:T(8,128)S(1)}, f32[200,128]{1,0:T(8,128)S(1)}, u32[]{:S(2)}, u32[]{:S(2)}) collective-permute-start(f32[200,128]{1,0:T(8,128)S(1)} %get-tuple-element.102), channel_id=1, source_target_pairs={{0,1},{1,0},{2,3},{3,2},{4,5},{5,4},{6,7},{7,6},{8,9},{9,8},{10,11... | collective-permute-start | bytes 307208 | tf_op jit(solution)/shard_map/ppermute | solution.py:429
  9.3 1.6 collective-permute-start.1
  10.9 3.0 %collective-permute-start.3 = (f32[200,128]{1,0:T(8,128)S(1)}, f32[200,128]{1,0:T(8,128)S(1)}, u32[]{:S(2)}, u32[]{:S(2)}) collective-permute-start(f32[200,128]{1,0:T(8,128)S(1)} %get-tuple-element.105), channel_id=1, source_target_pairs={{0,4},{1,5},{2,6},{3,7},{4,0},{5,1},{6,2},{7,3},{8,12},{9,13},{10,... | collective-permute-start | bytes 307208 | tf_op jit(solution)/shard_map/ppermute | solution.py:429
  15.2 3.6 %collective-permute-start.5 = (f32[200,128]{1,0:T(8,128)S(1)}, f32[200,128]{1,0:T(8,128)S(1)}, u32[]{:S(2)}, u32[]{:S(2)}) collective-permute-start(f32[200,128]{1,0:T(8,128)S(1)} %get-tuple-element.107), channel_id=1, source_target_pairs={{0,6},{1,7},{2,4},{3,5},{4,2},{5,3},{6,0},{7,1},{8,14},{9,15},{10,... | collective-permute-start | bytes 307208 | tf_op jit(solution)/shard_map/ppermute | solution.py:429
  18.9 2.4 %collective-permute-start.8 = (f32[200,128]{1,0:T(8,128)S(1)}, f32[200,128]{1,0:T(8,128)S(1)}, u32[]{:S(2)}, u32[]{:S(2)}) collective-permute-start(f32[200,128]{1,0:T(8,128)S(1)} %get-tuple-element.110), channel_id=1, source_target_pairs={{0,9},{1,8},{2,11},{3,10},{4,13},{5,12},{6,15},{7,14},{8,1},{9,0},... | collective-permute-start | bytes 307208 | tf_op jit(solution)/shard_map/ppermute | solution.py:429
  21.3 8.3 %collective-permute-done.4.refs_5_ = f32[200,128]{1,0:T(8,128)S(1)} collective-permute-done((f32[200,128]{1,0:T(8,128)S(1)}, f32[200,128]{1,0:T(8,128)S(1)}, u32[]{:S(2)}, u32[]{:S(2)}) %collective-permute-start.4) | collective-permute-done | bytes 102432 | tf_op jit(solution)/shard_map/ppermute | solution.py:429
  29.6 2.2 collective-permute-start.10
  31.8 1.9 collective-permute-start.11
  34.9 2.8 %collective-permute-start.13 = (f32[200,128]{1,0:T(8,128)S(1)}, f32[200,128]{1,0:T(8,128)S(1)}, u32[]{:S(2)}, u32[]{:S(2)}) collective-permute-start(f32[200,128]{1,0:T(8,128)S(1)} %get-tuple-element.115), channel_id=1, source_target_pairs={{0,14},{1,15},{2,12},{3,13},{4,10},{5,11},{6,8},{7,9},{8,6},{9,7},... | collective-permute-start | bytes 307208 | tf_op jit(solution)/shard_map/ppermute | solution.py:429
  38.9 1.5 collective-permute-start.15
  41.4 7.8 %collective-permute-done.12.refs_13_ = f32[200,128]{1,0:T(8,128)S(1)} collective-permute-done((f32[200,128]{1,0:T(8,128)S(1)}, f32[200,128]{1,0:T(8,128)S(1)}, u32[]{:S(2)}, u32[]{:S(2)}) %collective-permute-start.12) | collective-permute-done | bytes 102432 | tf_op jit(solution)/shard_map/ppermute | solution.py:429
  49.2 1.5 collective-permute-start.17
  50.7 2.2 collective-permute-start.18
  52.9 3.4 %collective-permute-start.19 = (f32[200,128]{1,0:T(8,128)S(1)}, f32[200,128]{1,0:T(8,128)S(1)}, u32[]{:S(2)}, u32[]{:S(2)}) collective-permute-start(f32[200,128]{1,0:T(8,128)S(1)} %get-tuple-element.121), channel_id=1, source_target_pairs={{0,20},{1,21},{2,22},{3,23},{4,16},{5,17},{6,18},{7,19},{8,28},{9,... | collective-permute-start | bytes 307208 | tf_op jit(solution)/shard_map/ppermute | solution.py:429
  57.7 2.9 %collective-permute-start.21 = (f32[200,128]{1,0:T(8,128)S(1)}, f32[200,128]{1,0:T(8,128)S(1)}, u32[]{:S(2)}, u32[]{:S(2)}) collective-permute-start(f32[200,128]{1,0:T(8,128)S(1)} %get-tuple-element.123), channel_id=1, source_target_pairs={{0,22},{1,23},{2,20},{3,21},{4,18},{5,19},{6,16},{7,17},{8,30},{9,... | collective-permute-start | bytes 307208 | tf_op jit(solution)/shard_map/ppermute | solution.py:429
  60.5 1.9 collective-permute-start.22
  62.4 7.1 %collective-permute-done.19.refs_20_ = f32[200,128]{1,0:T(8,128)S(1)} collective-permute-done((f32[200,128]{1,0:T(8,128)S(1)}, f32[200,128]{1,0:T(8,128)S(1)}, u32[]{:S(2)}, u32[]{:S(2)}) %collective-permute-start.19) | collective-permute-done | bytes 102432 | tf_op jit(solution)/shard_map/ppermute | solution.py:429
  69.6 2.2 collective-permute-done.20.refs_21_
  71.8 3.2 %collective-permute-start.26 = (f32[200,128]{1,0:T(8,128)S(1)}, f32[200,128]{1,0:T(8,128)S(1)}, u32[]{:S(2)}, u32[]{:S(2)}) collective-permute-start(f32[200,128]{1,0:T(8,128)S(1)} %get-tuple-element.128), channel_id=1, source_target_pairs={{0,27},{1,26},{2,25},{3,24},{4,31},{5,30},{6,29},{7,28},{8,19},{9,... | collective-permute-start | bytes 307208 | tf_op jit(solution)/shard_map/ppermute | solution.py:429
  75.0 2.2 collective-permute-start.27
  77.2 2.8 %collective-permute-start.28 = (f32[200,128]{1,0:T(8,128)S(1)}, f32[200,128]{1,0:T(8,128)S(1)}, u32[]{:S(2)}, u32[]{:S(2)}) collective-permute-start(f32[200,128]{1,0:T(8,128)S(1)} %get-tuple-element.130), channel_id=1, source_target_pairs={{0,29},{1,28},{2,31},{3,30},{4,25},{5,24},{6,27},{7,26},{8,21},{9,... | collective-permute-start | bytes 307208 | tf_op jit(solution)/shard_map/ppermute | solution.py:429
  80.0 3.0 %collective-permute-start.29 = (f32[200,128]{1,0:T(8,128)S(1)}, f32[200,128]{1,0:T(8,128)S(1)}, u32[]{:S(2)}, u32[]{:S(2)}) collective-permute-start(f32[200,128]{1,0:T(8,128)S(1)} %get-tuple-element.131), channel_id=1, source_target_pairs={{0,30},{1,31},{2,28},{3,29},{4,26},{5,27},{6,24},{7,25},{8,22},{9,... | collective-permute-start | bytes 307208 | tf_op jit(solution)/shard_map/ppermute | solution.py:429
  83.0 1.5 collective-permute-start.30
  84.5 9.6 %collective-permute-done.28.refs_29_ = f32[200,128]{1,0:T(8,128)S(1)} collective-permute-done((f32[200,128]{1,0:T(8,128)S(1)}, f32[200,128]{1,0:T(8,128)S(1)}, u32[]{:S(2)}, u32[]{:S(2)}) %collective-permute-start.28) | collective-permute-done | bytes 102432 | tf_op jit(solution)/shard_map/ppermute | solution.py:429
  94.1 3.0 %shard_map.147 = (f32[64,128]{1,0:T(8,128)S(1)}, f32[64,128]{1,0:T(8,128)S(1)}, f32[64,128]{1,0:T(8,128)S(1)}, f32[64,128]{1,0:T(8,128)S(1)}, f32[64,128]{1,0:T(...) custom-call(s32[1]{0:T(128)} %bitcast.me, ...), custom_call_target="tpu_custom_call" | custom-call | flops 1476395008 | bytes 2097152 | tf_op jit(solution)/shard_map/pallas_call | solution.py:225
  97.1 2.5 %collective-permute-start.62 = (f32[64,128]{1,0:T(8,128)S(1)}, f32[64,128]{1,0:T(8,128)S(1)}, u32[]{:S(2)}, u32[]{:S(2)}) collective-permute-start(f32[64,128]{1,0:T(8,128)S(1)} %get-tuple-element.166), channel_id=1, source_target_pairs={{0,1},{1,0},{2,3},{3,2},{4,5},{5,4},{6,7},{7,6},{8,9},{9,8},{10,11... | collective-permute-start | bytes 98312 | tf_op jit(solution)/shard_map/ppermute | solution.py:429
  99.6 4.6 %collective-permute-start.63 = (f32[64,128]{1,0:T(8,128)S(1)}, f32[64,128]{1,0:T(8,128)S(1)}, u32[]{:S(2)}, u32[]{:S(2)}) collective-permute-start(f32[64,128]{1,0:T(8,128)S(1)} %get-tuple-element.167), channel_id=1, source_target_pairs={{0,2},{1,3},{2,0},{3,1},{4,6},{5,7},{6,4},{7,5},{8,10},{9,11},{10,... | collective-permute-start | bytes 98312 | tf_op jit(solution)/shard_map/ppermute | solution.py:429
  104.2 2.6 %collective-permute-start.65 = (f32[64,128]{1,0:T(8,128)S(1)}, f32[64,128]{1,0:T(8,128)S(1)}, u32[]{:S(2)}, u32[]{:S(2)}) collective-permute-start(f32[64,128]{1,0:T(8,128)S(1)} %get-tuple-element.169), channel_id=1, source_target_pairs={{0,4},{1,5},{2,6},{3,7},{4,0},{5,1},{6,2},{7,3},{8,12},{9,13},{10,... | collective-permute-start | bytes 98312 | tf_op jit(solution)/shard_map/ppermute | solution.py:429
  108.1 2.3 collective-permute-start.67
  110.4 1.5 collective-permute-start.68
  111.9 1.6 collective-permute-start.70
  115.5 1.7 collective-permute-done.68.refs_7_
  117.3 2.5 %collective-permute-start.74 = (f32[64,128]{1,0:T(8,128)S(1)}, f32[64,128]{1,0:T(8,128)S(1)}, u32[]{:S(2)}, u32[]{:S(2)}) collective-permute-start(f32[64,128]{1,0:T(8,128)S(1)} %get-tuple-element.178), channel_id=1, source_target_pairs={{0,13},{1,12},{2,15},{3,14},{4,9},{5,8},{6,11},{7,10},{8,5},{9,4},... | collective-permute-start | bytes 98312 | tf_op jit(solution)/shard_map/ppermute | solution.py:429
  120.8 3.6 %collective-permute-start.76 = (f32[64,128]{1,0:T(8,128)S(1)}, f32[64,128]{1,0:T(8,128)S(1)}, u32[]{:S(2)}, u32[]{:S(2)}) collective-permute-start(f32[64,128]{1,0:T(8,128)S(1)} %get-tuple-element.180), channel_id=1, source_target_pairs={{0,15},{1,14},{2,13},{3,12},{4,11},{5,10},{6,9},{7,8},{8,7},{9,6},... | collective-permute-start | bytes 98312 | tf_op jit(solution)/shard_map/ppermute | solution.py:429
  124.7 1.6 collective-permute-start.78
  126.3 4.0 %collective-permute-start.80 = (f32[64,128]{1,0:T(8,128)S(1)}, f32[64,128]{1,0:T(8,128)S(1)}, u32[]{:S(2)}, u32[]{:S(2)}) collective-permute-start(f32[64,128]{1,0:T(8,128)S(1)} %get-tuple-element.184), channel_id=1, source_target_pairs={{0,19},{1,18},{2,17},{3,16},{4,23},{5,22},{6,21},{7,20},{8,27},{9,... | collective-permute-start | bytes 98312 | tf_op jit(solution)/shard_map/ppermute | solution.py:429
  130.2 3.7 %collective-permute-start.82 = (f32[64,128]{1,0:T(8,128)S(1)}, f32[64,128]{1,0:T(8,128)S(1)}, u32[]{:S(2)}, u32[]{:S(2)}) collective-permute-start(f32[64,128]{1,0:T(8,128)S(1)} %get-tuple-element.186), channel_id=1, source_target_pairs={{0,21},{1,20},{2,23},{3,22},{4,17},{5,16},{6,19},{7,18},{8,29},{9,... | collective-permute-start | bytes 98312 | tf_op jit(solution)/shard_map/ppermute | solution.py:429
  133.9 2.3 collective-permute-start.83
  136.2 3.5 %collective-permute-start.84 = (f32[64,128]{1,0:T(8,128)S(1)}, f32[64,128]{1,0:T(8,128)S(1)}, u32[]{:S(2)}, u32[]{:S(2)}) collective-permute-start(f32[64,128]{1,0:T(8,128)S(1)} %get-tuple-element.188), channel_id=1, source_target_pairs={{0,23},{1,22},{2,21},{3,20},{4,19},{5,18},{6,17},{7,16},{8,31},{9,... | collective-permute-start | bytes 98312 | tf_op jit(solution)/shard_map/ppermute | solution.py:429
  139.7 1.6 collective-permute-start.86
  141.3 3.7 %collective-permute-start.88 = (f32[64,128]{1,0:T(8,128)S(1)}, f32[64,128]{1,0:T(8,128)S(1)}, u32[]{:S(2)}, u32[]{:S(2)}) collective-permute-start(f32[64,128]{1,0:T(8,128)S(1)} %get-tuple-element.192), channel_id=1, source_target_pairs={{0,27},{1,26},{2,25},{3,24},{4,31},{5,30},{6,29},{7,28},{8,19},{9,... | collective-permute-start | bytes 98312 | tf_op jit(solution)/shard_map/ppermute | solution.py:429
  145.1 5.5 %shard_map.146 = (f32[128,128]{1,0:T(8,128)S(1)}, f32[128,128]{1,0:T(8,128)S(1)}, f32[128,128]{1,0:T(8,128)S(1)}, f32[128,128]{1,0:T(8,128)S(1)}, f32[128,128]{1...) custom-call(s32[1]{0:T(128)} %bitcast.me, ...), custom_call_target="tpu_custom_call" | custom-call | flops 2952790016 | bytes 4194304 | tf_op jit(solution)/shard_map/pallas_call | solution.py:225
  151.0 4.6 %collective-permute-start.90 = (f32[64,128]{1,0:T(8,128)S(1)}, f32[64,128]{1,0:T(8,128)S(1)}, u32[]{:S(2)}, u32[]{:S(2)}) collective-permute-start(f32[64,128]{1,0:T(8,128)S(1)} %get-tuple-element.194), channel_id=1, source_target_pairs={{0,29},{1,28},{2,31},{3,30},{4,25},{5,24},{6,27},{7,26},{8,21},{9,... | collective-permute-start | bytes 98312 | tf_op jit(solution)/shard_map/ppermute | solution.py:429
  156.2 3.7 %collective-permute-start.92 = (f32[64,128]{1,0:T(8,128)S(1)}, f32[64,128]{1,0:T(8,128)S(1)}, u32[]{:S(2)}, u32[]{:S(2)}) collective-permute-start(f32[64,128]{1,0:T(8,128)S(1)} %get-tuple-element.196), channel_id=1, source_target_pairs={{0,31},{1,30},{2,29},{3,28},{4,27},{5,26},{6,25},{7,24},{8,23},{9,... | collective-permute-start | bytes 98312 | tf_op jit(solution)/shard_map/ppermute | solution.py:429
  159.9 3.1 %collective-permute-start.33 = (f32[128,128]{1,0:T(8,128)S(1)}, f32[128,128]{1,0:T(8,128)S(1)}, u32[]{:S(2)}, u32[]{:S(2)}) collective-permute-start(f32[128,128]{1,0:T(8,128)S(1)} %get-tuple-element.136), channel_id=1, source_target_pairs={{0,3},{1,2},{2,1},{3,0},{4,7},{5,6},{6,5},{7,4},{8,11},{9,10},{10,... | collective-permute-start | bytes 196616 | tf_op jit(solution)/shard_map/ppermute | solution.py:429
  163.2 2.6 %collective-permute-start.35 = (f32[128,128]{1,0:T(8,128)S(1)}, f32[128,128]{1,0:T(8,128)S(1)}, u32[]{:S(2)}, u32[]{:S(2)}) collective-permute-start(f32[128,128]{1,0:T(8,128)S(1)} %get-tuple-element.138), channel_id=1, source_target_pairs={{0,5},{1,4},{2,7},{3,6},{4,1},{5,0},{6,3},{7,2},{8,13},{9,12},{10,... | collective-permute-start | bytes 196616 | tf_op jit(solution)/shard_map/ppermute | solution.py:429
  165.8 1.4 collective-permute-start.36
  167.2 3.4 %collective-permute-start.37 = (f32[128,128]{1,0:T(8,128)S(1)}, f32[128,128]{1,0:T(8,128)S(1)}, u32[]{:S(2)}, u32[]{:S(2)}) collective-permute-start(f32[128,128]{1,0:T(8,128)S(1)} %get-tuple-element.140), channel_id=1, source_target_pairs={{0,7},{1,6},{2,5},{3,4},{4,3},{5,2},{6,1},{7,0},{8,15},{9,14},{10,... | collective-permute-start | bytes 196616 | tf_op jit(solution)/shard_map/ppermute | solution.py:429
  171.2 2.2 collective-permute-done.35.refs_5_
  173.4 3.9 %collective-permute-start.41 = (f32[128,128]{1,0:T(8,128)S(1)}, f32[128,128]{1,0:T(8,128)S(1)}, u32[]{:S(2)}, u32[]{:S(2)}) collective-permute-start(f32[128,128]{1,0:T(8,128)S(1)} %get-tuple-element.144), channel_id=1, source_target_pairs={{0,11},{1,10},{2,9},{3,8},{4,15},{5,14},{6,13},{7,12},{8,3},{9,2},... | collective-permute-start | bytes 196616 | tf_op jit(solution)/shard_map/ppermute | solution.py:429
  178.7 2.4 %collective-permute-start.44 = (f32[128,128]{1,0:T(8,128)S(1)}, f32[128,128]{1,0:T(8,128)S(1)}, u32[]{:S(2)}, u32[]{:S(2)}) collective-permute-start(f32[128,128]{1,0:T(8,128)S(1)} %get-tuple-element.147), channel_id=1, source_target_pairs={{0,14},{1,15},{2,12},{3,13},{4,10},{5,11},{6,8},{7,9},{8,6},{9,7},... | collective-permute-start | bytes 196616 | tf_op jit(solution)/shard_map/ppermute | solution.py:429
  181.1 3.3 %collective-permute-start.45 = (f32[128,128]{1,0:T(8,128)S(1)}, f32[128,128]{1,0:T(8,128)S(1)}, u32[]{:S(2)}, u32[]{:S(2)}) collective-permute-start(f32[128,128]{1,0:T(8,128)S(1)} %get-tuple-element.148), channel_id=1, source_target_pairs={{0,15},{1,14},{2,13},{3,12},{4,11},{5,10},{6,9},{7,8},{8,7},{9,6},... | collective-permute-start | bytes 196616 | tf_op jit(solution)/shard_map/ppermute | solution.py:429
  184.4 3.5 %collective-permute-done.42.refs_12_ = f32[128,128]{1,0:T(8,128)S(1)} collective-permute-done((f32[128,128]{1,0:T(8,128)S(1)}, f32[128,128]{1,0:T(8,128)S(1)}, u32[]{:S(2)}, u32[]{:S(2)}) %collective-permute-start.42) | collective-permute-done | bytes 65568 | tf_op jit(solution)/shard_map/ppermute | solution.py:429
  189.2 3.8 %collective-permute-start.49 = (f32[128,128]{1,0:T(8,128)S(1)}, f32[128,128]{1,0:T(8,128)S(1)}, u32[]{:S(2)}, u32[]{:S(2)}) collective-permute-start(f32[128,128]{1,0:T(8,128)S(1)} %get-tuple-element.152), channel_id=1, source_target_pairs={{0,19},{1,18},{2,17},{3,16},{4,23},{5,22},{6,21},{7,20},{8,27},{9,... | collective-permute-start | bytes 196616 | tf_op jit(solution)/shard_map/ppermute | solution.py:429
  193.1 3.8 %collective-permute-start.51 = (f32[128,128]{1,0:T(8,128)S(1)}, f32[128,128]{1,0:T(8,128)S(1)}, u32[]{:S(2)}, u32[]{:S(2)}) collective-permute-start(f32[128,128]{1,0:T(8,128)S(1)} %get-tuple-element.154), channel_id=1, source_target_pairs={{0,21},{1,20},{2,23},{3,22},{4,17},{5,16},{6,19},{7,18},{8,29},{9,... | collective-permute-start | bytes 196616 | tf_op jit(solution)/shard_map/ppermute | solution.py:429
  198.0 4.5 %collective-permute-start.53 = (f32[128,128]{1,0:T(8,128)S(1)}, f32[128,128]{1,0:T(8,128)S(1)}, u32[]{:S(2)}, u32[]{:S(2)}) collective-permute-start(f32[128,128]{1,0:T(8,128)S(1)} %get-tuple-element.156), channel_id=1, source_target_pairs={{0,23},{1,22},{2,21},{3,20},{4,19},{5,18},{6,17},{7,16},{8,31},{9,... | collective-permute-start | bytes 196616 | tf_op jit(solution)/shard_map/ppermute | solution.py:429
  202.6 1.7 collective-permute-start.55
  204.9 3.0 %collective-permute-start.57 = (f32[128,128]{1,0:T(8,128)S(1)}, f32[128,128]{1,0:T(8,128)S(1)}, u32[]{:S(2)}, u32[]{:S(2)}) collective-permute-start(f32[128,128]{1,0:T(8,128)S(1)} %get-tuple-element.160), channel_id=1, source_target_pairs={{0,27},{1,26},{2,25},{3,24},{4,31},{5,30},{6,29},{7,28},{8,19},{9,... | collective-permute-start | bytes 196616 | tf_op jit(solution)/shard_map/ppermute | solution.py:429
  209.3 2.7 %collective-permute-start.59 = (f32[128,128]{1,0:T(8,128)S(1)}, f32[128,128]{1,0:T(8,128)S(1)}, u32[]{:S(2)}, u32[]{:S(2)}) collective-permute-start(f32[128,128]{1,0:T(8,128)S(1)} %get-tuple-element.162), channel_id=1, source_target_pairs={{0,29},{1,28},{2,31},{3,30},{4,25},{5,24},{6,27},{7,26},{8,21},{9,... | collective-permute-start | bytes 196616 | tf_op jit(solution)/shard_map/ppermute | solution.py:429
  212.6 4.2 %collective-permute-start.61 = (f32[128,128]{1,0:T(8,128)S(1)}, f32[128,128]{1,0:T(8,128)S(1)}, u32[]{:S(2)}, u32[]{:S(2)}) collective-permute-start(f32[128,128]{1,0:T(8,128)S(1)} %get-tuple-element.164), channel_id=1, source_target_pairs={{0,31},{1,30},{2,29},{3,28},{4,27},{5,26},{6,25},{7,24},{8,23},{9,... | collective-permute-start | bytes 196616 | tf_op jit(solution)/shard_map/ppermute | solution.py:429
  216.8 5.4 %shard_map.148.refs_33_ = f32[2,64,2048]{2,1,0:T(8,128)S(1)} custom-call(s32[1]{0:T(128)} %bitcast.me, f32[2,32,128]{2,1,0:T(8,128)S(1)} %copy-done.1, f32[64,128]{1,0:T(8,128)S(1)} %copy-done, f32[64,128]{1,0:T(8,128)S(1)} %get-tuple-element.165.refs_0_, f32[64,128]{1,0:T(8,128)S(1)} %collective-permute-done.62.refs_1_, ...), custom_call_target="tpu_custom_call" | custom-call | flops 201326592 | bytes 2097152 | tf_op jit(solution)/shard_map/pallas_call | solution.py:385
  222.2 5.7 %shard_map.149.refs_34_ = f32[2,64,2048]{2,1,0:T(8,128)S(1)} custom-call(s32[1]{0:T(128)} %bitcast.me, f32[2,32,128]{2,1,0:T(8,128)S(1)} %copy-done.1, f32[64,128]{1,0:T(8,128)S(1)} %copy-done, f32[128,128]{1,0:T(8,128)S(1)} %get-tuple-element.133.refs_0_, f32[128,128]{1,0:T(8,128)S(1)} %collective-permute-done.31.refs_1_, ...), custom_call_target="tpu_custom_call" | custom-call | flops 201326592 | bytes 2097152 | tf_op jit(solution)/shard_map/pallas_call | solution.py:385
  227.9 8.6 %shard_map.150 = f32[2,3,64,2048]{3,2,1,0:T(8,128)} custom-call(s32[1]{0:T(128)} %bitcast.me, f32[2,32,128]{2,1,0:T(8,128)S(1)} %copy-done.1, f32[64,128]{1,0:T(8,128)S(1)} %copy-done, f32[128,128]{1,0:T(8,128)S(1)} %get-tuple-element.133.refs_0_, f32[128,128]{1,0:T(8,128)S(1)} %collective-permute-done.31.refs_1_, ...), custom_call_target="tpu_custom_call" | custom-call | flops 210763776 | bytes 12582912 | tf_op jit(solution)/shard_map/pallas_call | solution.py:400
  (147 shorter events, 21.9 us)
Async XLA Ops:
  6.3 8.9 %collective-permute-start = (f32[200,128]{1,0:T(8,128)S(1)}, f32[200,128]{1,0:T(8,128)S(1)}, u32[]{:S(2)}, u32[]{:S(2)}) collective-permute-start(f32[200,128]{1,0:T(8,128)S(1)} %get-tuple-element.102), channel_id=1, source_target_pairs={{0,1},{1,0},{2,3},{3,2},{4,5},{5,4},{6,7},{7,6},{8,9},{9,8},{10,11... | collective-permute-start | bytes 307208 | tf_op jit(solution)/shard_map/ppermute | solution.py:429
  9.3 9.5 %collective-permute-start.1 = (f32[200,128]{1,0:T(8,128)S(1)}, f32[200,128]{1,0:T(8,128)S(1)}, u32[]{:S(2)}, u32[]{:S(2)}) collective-permute-start(f32[200,128]{1,0:T(8,128)S(1)} %get-tuple-element.103), channel_id=1, source_target_pairs={{0,2},{1,3},{2,0},{3,1},{4,6},{5,7},{6,4},{7,5},{8,10},{9,11},{10,... | collective-permute-start | bytes 307208 | tf_op jit(solution)/shard_map/ppermute | solution.py:429
  13.9 15.7 %collective-permute-start.4 = (f32[200,128]{1,0:T(8,128)S(1)}, f32[200,128]{1,0:T(8,128)S(1)}, u32[]{:S(2)}, u32[]{:S(2)}) collective-permute-start(f32[200,128]{1,0:T(8,128)S(1)} %get-tuple-element.106), channel_id=1, source_target_pairs={{0,5},{1,4},{2,7},{3,6},{4,1},{5,0},{6,3},{7,2},{8,13},{9,12},{10,... | collective-permute-start | bytes 307208 | tf_op jit(solution)/shard_map/ppermute | solution.py:429
  15.2 14.4 %collective-permute-start.5 = (f32[200,128]{1,0:T(8,128)S(1)}, f32[200,128]{1,0:T(8,128)S(1)}, u32[]{:S(2)}, u32[]{:S(2)}) collective-permute-start(f32[200,128]{1,0:T(8,128)S(1)} %get-tuple-element.107), channel_id=1, source_target_pairs={{0,6},{1,7},{2,4},{3,5},{4,2},{5,3},{6,0},{7,1},{8,14},{9,15},{10,... | collective-permute-start | bytes 307208 | tf_op jit(solution)/shard_map/ppermute | solution.py:429
  18.8 13.0 %collective-permute-start.6 = (f32[200,128]{1,0:T(8,128)S(1)}, f32[200,128]{1,0:T(8,128)S(1)}, u32[]{:S(2)}, u32[]{:S(2)}) collective-permute-start(f32[200,128]{1,0:T(8,128)S(1)} %get-tuple-element.108), channel_id=1, source_target_pairs={{0,7},{1,6},{2,5},{3,4},{4,3},{5,2},{6,1},{7,0},{8,15},{9,14},{10,... | collective-permute-start | bytes 307208 | tf_op jit(solution)/shard_map/ppermute | solution.py:429
  18.8 14.8 %collective-permute-start.7 = (f32[200,128]{1,0:T(8,128)S(1)}, f32[200,128]{1,0:T(8,128)S(1)}, u32[]{:S(2)}, u32[]{:S(2)}) collective-permute-start(f32[200,128]{1,0:T(8,128)S(1)} %get-tuple-element.109), channel_id=1, source_target_pairs={{0,8},{1,9},{2,10},{3,11},{4,12},{5,13},{6,14},{7,15},{8,0},{9,1},... | collective-permute-start | bytes 307208 | tf_op jit(solution)/shard_map/ppermute | solution.py:429
  18.9 16.0 %collective-permute-start.8 = (f32[200,128]{1,0:T(8,128)S(1)}, f32[200,128]{1,0:T(8,128)S(1)}, u32[]{:S(2)}, u32[]{:S(2)}) collective-permute-start(f32[200,128]{1,0:T(8,128)S(1)} %get-tuple-element.110), channel_id=1, source_target_pairs={{0,9},{1,8},{2,11},{3,10},{4,13},{5,12},{6,15},{7,14},{8,1},{9,0},... | collective-permute-start | bytes 307208 | tf_op jit(solution)/shard_map/ppermute | solution.py:429
  29.6 9.3 %collective-permute-start.10 = (f32[200,128]{1,0:T(8,128)S(1)}, f32[200,128]{1,0:T(8,128)S(1)}, u32[]{:S(2)}, u32[]{:S(2)}) collective-permute-start(f32[200,128]{1,0:T(8,128)S(1)} %get-tuple-element.112), channel_id=1, source_target_pairs={{0,11},{1,10},{2,9},{3,8},{4,15},{5,14},{6,13},{7,12},{8,3},{9,2},... | collective-permute-start | bytes 307208 | tf_op jit(solution)/shard_map/ppermute | solution.py:429
  33.7 15.5 %collective-permute-start.12 = (f32[200,128]{1,0:T(8,128)S(1)}, f32[200,128]{1,0:T(8,128)S(1)}, u32[]{:S(2)}, u32[]{:S(2)}) collective-permute-start(f32[200,128]{1,0:T(8,128)S(1)} %get-tuple-element.114), channel_id=1, source_target_pairs={{0,13},{1,12},{2,15},{3,14},{4,9},{5,8},{6,11},{7,10},{8,5},{9,4},... | collective-permute-start | bytes 307208 | tf_op jit(solution)/shard_map/ppermute | solution.py:429
  34.9 15.8 %collective-permute-start.13 = (f32[200,128]{1,0:T(8,128)S(1)}, f32[200,128]{1,0:T(8,128)S(1)}, u32[]{:S(2)}, u32[]{:S(2)}) collective-permute-start(f32[200,128]{1,0:T(8,128)S(1)} %get-tuple-element.115), channel_id=1, source_target_pairs={{0,14},{1,15},{2,12},{3,13},{4,10},{5,11},{6,8},{7,9},{8,6},{9,7},... | collective-permute-start | bytes 307208 | tf_op jit(solution)/shard_map/ppermute | solution.py:429
  37.7 15.2 %collective-permute-start.14 = (f32[200,128]{1,0:T(8,128)S(1)}, f32[200,128]{1,0:T(8,128)S(1)}, u32[]{:S(2)}, u32[]{:S(2)}) collective-permute-start(f32[200,128]{1,0:T(8,128)S(1)} %get-tuple-element.116), channel_id=1, source_target_pairs={{0,15},{1,14},{2,13},{3,12},{4,11},{5,10},{6,9},{7,8},{8,7},{9,6},... | collective-permute-start | bytes 307208 | tf_op jit(solution)/shard_map/ppermute | solution.py:429
  38.9 17.5 %collective-permute-start.15 = (f32[200,128]{1,0:T(8,128)S(1)}, f32[200,128]{1,0:T(8,128)S(1)}, u32[]{:S(2)}, u32[]{:S(2)}) collective-permute-start(f32[200,128]{1,0:T(8,128)S(1)} %get-tuple-element.117), channel_id=1, source_target_pairs={{0,16},{1,17},{2,18},{3,19},{4,20},{5,21},{6,22},{7,23},{8,24},{9,... | collective-permute-start | bytes 307208 | tf_op jit(solution)/shard_map/ppermute | solution.py:429
  40.4 17.3 %collective-permute-start.16 = (f32[200,128]{1,0:T(8,128)S(1)}, f32[200,128]{1,0:T(8,128)S(1)}, u32[]{:S(2)}, u32[]{:S(2)}) collective-permute-start(f32[200,128]{1,0:T(8,128)S(1)} %get-tuple-element.118), channel_id=1, source_target_pairs={{0,17},{1,16},{2,19},{3,18},{4,21},{5,20},{6,23},{7,22},{8,25},{9,... | collective-permute-start | bytes 307208 | tf_op jit(solution)/shard_map/ppermute | solution.py:429
  49.2 11.3 %collective-permute-start.17 = (f32[200,128]{1,0:T(8,128)S(1)}, f32[200,128]{1,0:T(8,128)S(1)}, u32[]{:S(2)}, u32[]{:S(2)}) collective-permute-start(f32[200,128]{1,0:T(8,128)S(1)} %get-tuple-element.119), channel_id=1, source_target_pairs={{0,18},{1,19},{2,16},{3,17},{4,22},{5,23},{6,20},{7,21},{8,26},{9,... | collective-permute-start | bytes 307208 | tf_op jit(solution)/shard_map/ppermute | solution.py:429
  50.7 11.7 %collective-permute-start.18 = (f32[200,128]{1,0:T(8,128)S(1)}, f32[200,128]{1,0:T(8,128)S(1)}, u32[]{:S(2)}, u32[]{:S(2)}) collective-permute-start(f32[200,128]{1,0:T(8,128)S(1)} %get-tuple-element.120), channel_id=1, source_target_pairs={{0,19},{1,18},{2,17},{3,16},{4,23},{5,22},{6,21},{7,20},{8,27},{9,... | collective-permute-start | bytes 307208 | tf_op jit(solution)/shard_map/ppermute | solution.py:429
  52.9 16.6 %collective-permute-start.19 = (f32[200,128]{1,0:T(8,128)S(1)}, f32[200,128]{1,0:T(8,128)S(1)}, u32[]{:S(2)}, u32[]{:S(2)}) collective-permute-start(f32[200,128]{1,0:T(8,128)S(1)} %get-tuple-element.121), channel_id=1, source_target_pairs={{0,20},{1,21},{2,22},{3,23},{4,16},{5,17},{6,18},{7,19},{8,28},{9,... | collective-permute-start | bytes 307208 | tf_op jit(solution)/shard_map/ppermute | solution.py:429
  56.3 15.4 %collective-permute-start.20 = (f32[200,128]{1,0:T(8,128)S(1)}, f32[200,128]{1,0:T(8,128)S(1)}, u32[]{:S(2)}, u32[]{:S(2)}) collective-permute-start(f32[200,128]{1,0:T(8,128)S(1)} %get-tuple-element.122), channel_id=1, source_target_pairs={{0,21},{1,20},{2,23},{3,22},{4,17},{5,16},{6,19},{7,18},{8,29},{9,... | collective-permute-start | bytes 307208 | tf_op jit(solution)/shard_map/ppermute | solution.py:429
  57.7 14.1 %collective-permute-start.21 = (f32[200,128]{1,0:T(8,128)S(1)}, f32[200,128]{1,0:T(8,128)S(1)}, u32[]{:S(2)}, u32[]{:S(2)}) collective-permute-start(f32[200,128]{1,0:T(8,128)S(1)} %get-tuple-element.123), channel_id=1, source_target_pairs={{0,22},{1,23},{2,20},{3,21},{4,18},{5,19},{6,16},{7,17},{8,30},{9,... | collective-permute-start | bytes 307208 | tf_op jit(solution)/shard_map/ppermute | solution.py:429
  60.5 14.5 %collective-permute-start.22 = (f32[200,128]{1,0:T(8,128)S(1)}, f32[200,128]{1,0:T(8,128)S(1)}, u32[]{:S(2)}, u32[]{:S(2)}) collective-permute-start(f32[200,128]{1,0:T(8,128)S(1)} %get-tuple-element.124), channel_id=1, source_target_pairs={{0,23},{1,22},{2,21},{3,20},{4,19},{5,18},{6,17},{7,16},{8,31},{9,... | collective-permute-start | bytes 307208 | tf_op jit(solution)/shard_map/ppermute | solution.py:429
  62.4 14.8 %collective-permute-start.23 = (f32[200,128]{1,0:T(8,128)S(1)}, f32[200,128]{1,0:T(8,128)S(1)}, u32[]{:S(2)}, u32[]{:S(2)}) collective-permute-start(f32[200,128]{1,0:T(8,128)S(1)} %get-tuple-element.125), channel_id=1, source_target_pairs={{0,24},{1,25},{2,26},{3,27},{4,28},{5,29},{6,30},{7,31},{8,16},{9,... | collective-permute-start | bytes 307208 | tf_op jit(solution)/shard_map/ppermute | solution.py:429
  69.6 10.4 %collective-permute-start.24 = (f32[200,128]{1,0:T(8,128)S(1)}, f32[200,128]{1,0:T(8,128)S(1)}, u32[]{:S(2)}, u32[]{:S(2)}) collective-permute-start(f32[200,128]{1,0:T(8,128)S(1)} %get-tuple-element.126), channel_id=1, source_target_pairs={{0,25},{1,24},{2,27},{3,26},{4,29},{5,28},{6,31},{7,30},{8,17},{9,... | collective-permute-start | bytes 307208 | tf_op jit(solution)/shard_map/ppermute | solution.py:429
  71.8 11.2 %collective-permute-start.25 = (f32[200,128]{1,0:T(8,128)S(1)}, f32[200,128]{1,0:T(8,128)S(1)}, u32[]{:S(2)}, u32[]{:S(2)}) collective-permute-start(f32[200,128]{1,0:T(8,128)S(1)} %get-tuple-element.127), channel_id=1, source_target_pairs={{0,26},{1,27},{2,24},{3,25},{4,30},{5,31},{6,28},{7,29},{8,18},{9,... | collective-permute-start | bytes 307208 | tf_op jit(solution)/shard_map/ppermute | solution.py:429
  71.8 12.7 %collective-permute-start.26 = (f32[200,128]{1,0:T(8,128)S(1)}, f32[200,128]{1,0:T(8,128)S(1)}, u32[]{:S(2)}, u32[]{:S(2)}) collective-permute-start(f32[200,128]{1,0:T(8,128)S(1)} %get-tuple-element.128), channel_id=1, source_target_pairs={{0,27},{1,26},{2,25},{3,24},{4,31},{5,30},{6,29},{7,28},{8,19},{9,... | collective-permute-start | bytes 307208 | tf_op jit(solution)/shard_map/ppermute | solution.py:429
  75.0 9.5 %collective-permute-start.27 = (f32[200,128]{1,0:T(8,128)S(1)}, f32[200,128]{1,0:T(8,128)S(1)}, u32[]{:S(2)}, u32[]{:S(2)}) collective-permute-start(f32[200,128]{1,0:T(8,128)S(1)} %get-tuple-element.129), channel_id=1, source_target_pairs={{0,28},{1,29},{2,30},{3,31},{4,24},{5,25},{6,26},{7,27},{8,20},{9,... | collective-permute-start | bytes 307208 | tf_op jit(solution)/shard_map/ppermute | solution.py:429
  77.2 16.9 %collective-permute-start.28 = (f32[200,128]{1,0:T(8,128)S(1)}, f32[200,128]{1,0:T(8,128)S(1)}, u32[]{:S(2)}, u32[]{:S(2)}) collective-permute-start(f32[200,128]{1,0:T(8,128)S(1)} %get-tuple-element.130), channel_id=1, source_target_pairs={{0,29},{1,28},{2,31},{3,30},{4,25},{5,24},{6,27},{7,26},{8,21},{9,... | collective-permute-start | bytes 307208 | tf_op jit(solution)/shard_map/ppermute | solution.py:429
  80.0 14.1 %collective-permute-start.29 = (f32[200,128]{1,0:T(8,128)S(1)}, f32[200,128]{1,0:T(8,128)S(1)}, u32[]{:S(2)}, u32[]{:S(2)}) collective-permute-start(f32[200,128]{1,0:T(8,128)S(1)} %get-tuple-element.131), channel_id=1, source_target_pairs={{0,30},{1,31},{2,28},{3,29},{4,26},{5,27},{6,24},{7,25},{8,22},{9,... | collective-permute-start | bytes 307208 | tf_op jit(solution)/shard_map/ppermute | solution.py:429
  83.0 11.1 %collective-permute-start.30 = (f32[200,128]{1,0:T(8,128)S(1)}, f32[200,128]{1,0:T(8,128)S(1)}, u32[]{:S(2)}, u32[]{:S(2)}) collective-permute-start(f32[200,128]{1,0:T(8,128)S(1)} %get-tuple-element.132), channel_id=1, source_target_pairs={{0,31},{1,30},{2,29},{3,28},{4,27},{5,26},{6,25},{7,24},{8,23},{9,... | collective-permute-start | bytes 307208 | tf_op jit(solution)/shard_map/ppermute | solution.py:429
  97.1 10.9 %collective-permute-start.62 = (f32[64,128]{1,0:T(8,128)S(1)}, f32[64,128]{1,0:T(8,128)S(1)}, u32[]{:S(2)}, u32[]{:S(2)}) collective-permute-start(f32[64,128]{1,0:T(8,128)S(1)} %get-tuple-element.166), channel_id=1, source_target_pairs={{0,1},{1,0},{2,3},{3,2},{4,5},{5,4},{6,7},{7,6},{8,9},{9,8},{10,11... | collective-permute-start | bytes 98312 | tf_op jit(solution)/shard_map/ppermute | solution.py:429
  99.6 10.8 %collective-permute-start.63 = (f32[64,128]{1,0:T(8,128)S(1)}, f32[64,128]{1,0:T(8,128)S(1)}, u32[]{:S(2)}, u32[]{:S(2)}) collective-permute-start(f32[64,128]{1,0:T(8,128)S(1)} %get-tuple-element.167), channel_id=1, source_target_pairs={{0,2},{1,3},{2,0},{3,1},{4,6},{5,7},{6,4},{7,5},{8,10},{9,11},{10,... | collective-permute-start | bytes 98312 | tf_op jit(solution)/shard_map/ppermute | solution.py:429
  114.1 10.3 %collective-permute-start.72 = (f32[64,128]{1,0:T(8,128)S(1)}, f32[64,128]{1,0:T(8,128)S(1)}, u32[]{:S(2)}, u32[]{:S(2)}) collective-permute-start(f32[64,128]{1,0:T(8,128)S(1)} %get-tuple-element.176), channel_id=1, source_target_pairs={{0,11},{1,10},{2,9},{3,8},{4,15},{5,14},{6,13},{7,12},{8,3},{9,2},... | collective-permute-start | bytes 98312 | tf_op jit(solution)/shard_map/ppermute | solution.py:429
  117.3 9.0 %collective-permute-start.74 = (f32[64,128]{1,0:T(8,128)S(1)}, f32[64,128]{1,0:T(8,128)S(1)}, u32[]{:S(2)}, u32[]{:S(2)}) collective-permute-start(f32[64,128]{1,0:T(8,128)S(1)} %get-tuple-element.178), channel_id=1, source_target_pairs={{0,13},{1,12},{2,15},{3,14},{4,9},{5,8},{6,11},{7,10},{8,5},{9,4},... | collective-permute-start | bytes 98312 | tf_op jit(solution)/shard_map/ppermute | solution.py:429
  120.8 9.4 %collective-permute-start.76 = (f32[64,128]{1,0:T(8,128)S(1)}, f32[64,128]{1,0:T(8,128)S(1)}, u32[]{:S(2)}, u32[]{:S(2)}) collective-permute-start(f32[64,128]{1,0:T(8,128)S(1)} %get-tuple-element.180), channel_id=1, source_target_pairs={{0,15},{1,14},{2,13},{3,12},{4,11},{5,10},{6,9},{7,8},{8,7},{9,6},... | collective-permute-start | bytes 98312 | tf_op jit(solution)/shard_map/ppermute | solution.py:429
  124.7 9.2 %collective-permute-start.78 = (f32[64,128]{1,0:T(8,128)S(1)}, f32[64,128]{1,0:T(8,128)S(1)}, u32[]{:S(2)}, u32[]{:S(2)}) collective-permute-start(f32[64,128]{1,0:T(8,128)S(1)} %get-tuple-element.182), channel_id=1, source_target_pairs={{0,17},{1,16},{2,19},{3,18},{4,21},{5,20},{6,23},{7,22},{8,25},{9,... | collective-permute-start | bytes 98312 | tf_op jit(solution)/shard_map/ppermute | solution.py:429
  126.2 9.9 %collective-permute-start.79 = (f32[64,128]{1,0:T(8,128)S(1)}, f32[64,128]{1,0:T(8,128)S(1)}, u32[]{:S(2)}, u32[]{:S(2)}) collective-permute-start(f32[64,128]{1,0:T(8,128)S(1)} %get-tuple-element.183), channel_id=1, source_target_pairs={{0,18},{1,19},{2,16},{3,17},{4,22},{5,23},{6,20},{7,21},{8,26},{9,... | collective-permute-start | bytes 98312 | tf_op jit(solution)/shard_map/ppermute | solution.py:429
  126.3 13.4 %collective-permute-start.80 = (f32[64,128]{1,0:T(8,128)S(1)}, f32[64,128]{1,0:T(8,128)S(1)}, u32[]{:S(2)}, u32[]{:S(2)}) collective-permute-start(f32[64,128]{1,0:T(8,128)S(1)} %get-tuple-element.184), channel_id=1, source_target_pairs={{0,19},{1,18},{2,17},{3,16},{4,23},{5,22},{6,21},{7,20},{8,27},{9,... | collective-permute-start | bytes 98312 | tf_op jit(solution)/shard_map/ppermute | solution.py:429
  130.2 9.5 %collective-permute-start.81 = (f32[64,128]{1,0:T(8,128)S(1)}, f32[64,128]{1,0:T(8,128)S(1)}, u32[]{:S(2)}, u32[]{:S(2)}) collective-permute-start(f32[64,128]{1,0:T(8,128)S(1)} %get-tuple-element.185), channel_id=1, source_target_pairs={{0,20},{1,21},{2,22},{3,23},{4,16},{5,17},{6,18},{7,19},{8,28},{9,... | collective-permute-start | bytes 98312 | tf_op jit(solution)/shard_map/ppermute | solution.py:429
  130.2 11.1 %collective-permute-start.82 = (f32[64,128]{1,0:T(8,128)S(1)}, f32[64,128]{1,0:T(8,128)S(1)}, u32[]{:S(2)}, u32[]{:S(2)}) collective-permute-start(f32[64,128]{1,0:T(8,128)S(1)} %get-tuple-element.186), channel_id=1, source_target_pairs={{0,21},{1,20},{2,23},{3,22},{4,17},{5,16},{6,19},{7,18},{8,29},{9,... | collective-permute-start | bytes 98312 | tf_op jit(solution)/shard_map/ppermute | solution.py:429
  136.2 14.4 %collective-permute-start.84 = (f32[64,128]{1,0:T(8,128)S(1)}, f32[64,128]{1,0:T(8,128)S(1)}, u32[]{:S(2)}, u32[]{:S(2)}) collective-permute-start(f32[64,128]{1,0:T(8,128)S(1)} %get-tuple-element.188), channel_id=1, source_target_pairs={{0,23},{1,22},{2,21},{3,20},{4,19},{5,18},{6,17},{7,16},{8,31},{9,... | collective-permute-start | bytes 98312 | tf_op jit(solution)/shard_map/ppermute | solution.py:429
  139.7 11.4 %collective-permute-start.85 = (f32[64,128]{1,0:T(8,128)S(1)}, f32[64,128]{1,0:T(8,128)S(1)}, u32[]{:S(2)}, u32[]{:S(2)}) collective-permute-start(f32[64,128]{1,0:T(8,128)S(1)} %get-tuple-element.189), channel_id=1, source_target_pairs={{0,24},{1,25},{2,26},{3,27},{4,28},{5,29},{6,30},{7,31},{8,16},{9,... | collective-permute-start | bytes 98312 | tf_op jit(solution)/shard_map/ppermute | solution.py:429
  139.7 11.4 %collective-permute-start.86 = (f32[64,128]{1,0:T(8,128)S(1)}, f32[64,128]{1,0:T(8,128)S(1)}, u32[]{:S(2)}, u32[]{:S(2)}) collective-permute-start(f32[64,128]{1,0:T(8,128)S(1)} %get-tuple-element.190), channel_id=1, source_target_pairs={{0,25},{1,24},{2,27},{3,26},{4,29},{5,28},{6,31},{7,30},{8,17},{9,... | collective-permute-start | bytes 98312 | tf_op jit(solution)/shard_map/ppermute | solution.py:429
  141.3 14.3 %collective-permute-start.87 = (f32[64,128]{1,0:T(8,128)S(1)}, f32[64,128]{1,0:T(8,128)S(1)}, u32[]{:S(2)}, u32[]{:S(2)}) collective-permute-start(f32[64,128]{1,0:T(8,128)S(1)} %get-tuple-element.191), channel_id=1, source_target_pairs={{0,26},{1,27},{2,24},{3,25},{4,30},{5,31},{6,28},{7,29},{8,18},{9,... | collective-permute-start | bytes 98312 | tf_op jit(solution)/shard_map/ppermute | solution.py:429
  141.3 14.9 %collective-permute-start.88 = (f32[64,128]{1,0:T(8,128)S(1)}, f32[64,128]{1,0:T(8,128)S(1)}, u32[]{:S(2)}, u32[]{:S(2)}) collective-permute-start(f32[64,128]{1,0:T(8,128)S(1)} %get-tuple-element.192), channel_id=1, source_target_pairs={{0,27},{1,26},{2,25},{3,24},{4,31},{5,30},{6,29},{7,28},{8,19},{9,... | collective-permute-start | bytes 98312 | tf_op jit(solution)/shard_map/ppermute | solution.py:429
  150.5 15.3 %collective-permute-start.31 = (f32[128,128]{1,0:T(8,128)S(1)}, f32[128,128]{1,0:T(8,128)S(1)}, u32[]{:S(2)}, u32[]{:S(2)}) collective-permute-start(f32[128,128]{1,0:T(8,128)S(1)} %get-tuple-element.134), channel_id=1, source_target_pairs={{0,1},{1,0},{2,3},{3,2},{4,5},{5,4},{6,7},{7,6},{8,9},{9,8},{10,11... | collective-permute-start | bytes 196616 | tf_op jit(solution)/shard_map/ppermute | solution.py:429
  151.0 8.9 %collective-permute-start.89 = (f32[64,128]{1,0:T(8,128)S(1)}, f32[64,128]{1,0:T(8,128)S(1)}, u32[]{:S(2)}, u32[]{:S(2)}) collective-permute-start(f32[64,128]{1,0:T(8,128)S(1)} %get-tuple-element.193), channel_id=1, source_target_pairs={{0,28},{1,29},{2,30},{3,31},{4,24},{5,25},{6,26},{7,27},{8,20},{9,... | collective-permute-start | bytes 98312 | tf_op jit(solution)/shard_map/ppermute | solution.py:429
  151.0 8.9 %collective-permute-start.90 = (f32[64,128]{1,0:T(8,128)S(1)}, f32[64,128]{1,0:T(8,128)S(1)}, u32[]{:S(2)}, u32[]{:S(2)}) collective-permute-start(f32[64,128]{1,0:T(8,128)S(1)} %get-tuple-element.194), channel_id=1, source_target_pairs={{0,29},{1,28},{2,31},{3,30},{4,25},{5,24},{6,27},{7,26},{8,21},{9,... | collective-permute-start | bytes 98312 | tf_op jit(solution)/shard_map/ppermute | solution.py:429
  159.9 10.7 %collective-permute-start.33 = (f32[128,128]{1,0:T(8,128)S(1)}, f32[128,128]{1,0:T(8,128)S(1)}, u32[]{:S(2)}, u32[]{:S(2)}) collective-permute-start(f32[128,128]{1,0:T(8,128)S(1)} %get-tuple-element.136), channel_id=1, source_target_pairs={{0,3},{1,2},{2,1},{3,0},{4,7},{5,6},{6,5},{7,4},{8,11},{9,10},{10,... | collective-permute-start | bytes 196616 | tf_op jit(solution)/shard_map/ppermute | solution.py:429
  163.2 10.2 %collective-permute-start.35 = (f32[128,128]{1,0:T(8,128)S(1)}, f32[128,128]{1,0:T(8,128)S(1)}, u32[]{:S(2)}, u32[]{:S(2)}) collective-permute-start(f32[128,128]{1,0:T(8,128)S(1)} %get-tuple-element.138), channel_id=1, source_target_pairs={{0,5},{1,4},{2,7},{3,6},{4,1},{5,0},{6,3},{7,2},{8,13},{9,12},{10,... | collective-permute-start | bytes 196616 | tf_op jit(solution)/shard_map/ppermute | solution.py:429
  167.2 10.0 %collective-permute-start.37 = (f32[128,128]{1,0:T(8,128)S(1)}, f32[128,128]{1,0:T(8,128)S(1)}, u32[]{:S(2)}, u32[]{:S(2)}) collective-permute-start(f32[128,128]{1,0:T(8,128)S(1)} %get-tuple-element.140), channel_id=1, source_target_pairs={{0,7},{1,6},{2,5},{3,4},{4,3},{5,2},{6,1},{7,0},{8,15},{9,14},{10,... | collective-permute-start | bytes 196616 | tf_op jit(solution)/shard_map/ppermute | solution.py:429
  173.4 11.0 %collective-permute-start.41 = (f32[128,128]{1,0:T(8,128)S(1)}, f32[128,128]{1,0:T(8,128)S(1)}, u32[]{:S(2)}, u32[]{:S(2)}) collective-permute-start(f32[128,128]{1,0:T(8,128)S(1)} %get-tuple-element.144), channel_id=1, source_target_pairs={{0,11},{1,10},{2,9},{3,8},{4,15},{5,14},{6,13},{7,12},{8,3},{9,2},... | collective-permute-start | bytes 196616 | tf_op jit(solution)/shard_map/ppermute | solution.py:429
  177.3 10.6 %collective-permute-start.42 = (f32[128,128]{1,0:T(8,128)S(1)}, f32[128,128]{1,0:T(8,128)S(1)}, u32[]{:S(2)}, u32[]{:S(2)}) collective-permute-start(f32[128,128]{1,0:T(8,128)S(1)} %get-tuple-element.145), channel_id=1, source_target_pairs={{0,12},{1,13},{2,14},{3,15},{4,8},{5,9},{6,10},{7,11},{8,4},{9,5},... | collective-permute-start | bytes 196616 | tf_op jit(solution)/shard_map/ppermute | solution.py:429
  177.6 11.6 %collective-permute-start.43 = (f32[128,128]{1,0:T(8,128)S(1)}, f32[128,128]{1,0:T(8,128)S(1)}, u32[]{:S(2)}, u32[]{:S(2)}) collective-permute-start(f32[128,128]{1,0:T(8,128)S(1)} %get-tuple-element.146), channel_id=1, source_target_pairs={{0,13},{1,12},{2,15},{3,14},{4,9},{5,8},{6,11},{7,10},{8,5},{9,4},... | collective-permute-start | bytes 196616 | tf_op jit(solution)/shard_map/ppermute | solution.py:429
  178.7 10.5 %collective-permute-start.44 = (f32[128,128]{1,0:T(8,128)S(1)}, f32[128,128]{1,0:T(8,128)S(1)}, u32[]{:S(2)}, u32[]{:S(2)}) collective-permute-start(f32[128,128]{1,0:T(8,128)S(1)} %get-tuple-element.147), channel_id=1, source_target_pairs={{0,14},{1,15},{2,12},{3,13},{4,10},{5,11},{6,8},{7,9},{8,6},{9,7},... | collective-permute-start | bytes 196616 | tf_op jit(solution)/shard_map/ppermute | solution.py:429
  181.1 12.0 %collective-permute-start.45 = (f32[128,128]{1,0:T(8,128)S(1)}, f32[128,128]{1,0:T(8,128)S(1)}, u32[]{:S(2)}, u32[]{:S(2)}) collective-permute-start(f32[128,128]{1,0:T(8,128)S(1)} %get-tuple-element.148), channel_id=1, source_target_pairs={{0,15},{1,14},{2,13},{3,12},{4,11},{5,10},{6,9},{7,8},{8,7},{9,6},... | collective-permute-start | bytes 196616 | tf_op jit(solution)/shard_map/ppermute | solution.py:429
  187.8 9.0 %collective-permute-start.47 = (f32[128,128]{1,0:T(8,128)S(1)}, f32[128,128]{1,0:T(8,128)S(1)}, u32[]{:S(2)}, u32[]{:S(2)}) collective-permute-start(f32[128,128]{1,0:T(8,128)S(1)} %get-tuple-element.150), channel_id=1, source_target_pairs={{0,17},{1,16},{2,19},{3,18},{4,21},{5,20},{6,23},{7,22},{8,25},{9,... | collective-permute-start | bytes 196616 | tf_op jit(solution)/shard_map/ppermute | solution.py:429
  189.2 13.3 %collective-permute-start.49 = (f32[128,128]{1,0:T(8,128)S(1)}, f32[128,128]{1,0:T(8,128)S(1)}, u32[]{:S(2)}, u32[]{:S(2)}) collective-permute-start(f32[128,128]{1,0:T(8,128)S(1)} %get-tuple-element.152), channel_id=1, source_target_pairs={{0,19},{1,18},{2,17},{3,16},{4,23},{5,22},{6,21},{7,20},{8,27},{9,... | collective-permute-start | bytes 196616 | tf_op jit(solution)/shard_map/ppermute | solution.py:429
  193.1 9.5 %collective-permute-start.50 = (f32[128,128]{1,0:T(8,128)S(1)}, f32[128,128]{1,0:T(8,128)S(1)}, u32[]{:S(2)}, u32[]{:S(2)}) collective-permute-start(f32[128,128]{1,0:T(8,128)S(1)} %get-tuple-element.153), channel_id=1, source_target_pairs={{0,20},{1,21},{2,22},{3,23},{4,16},{5,17},{6,18},{7,19},{8,28},{9,... | collective-permute-start | bytes 196616 | tf_op jit(solution)/shard_map/ppermute | solution.py:429
  193.1 11.8 %collective-permute-start.51 = (f32[128,128]{1,0:T(8,128)S(1)}, f32[128,128]{1,0:T(8,128)S(1)}, u32[]{:S(2)}, u32[]{:S(2)}) collective-permute-start(f32[128,128]{1,0:T(8,128)S(1)} %get-tuple-element.154), channel_id=1, source_target_pairs={{0,21},{1,20},{2,23},{3,22},{4,17},{5,16},{6,19},{7,18},{8,29},{9,... | collective-permute-start | bytes 196616 | tf_op jit(solution)/shard_map/ppermute | solution.py:429
  198.0 9.8 %collective-permute-start.53 = (f32[128,128]{1,0:T(8,128)S(1)}, f32[128,128]{1,0:T(8,128)S(1)}, u32[]{:S(2)}, u32[]{:S(2)}) collective-permute-start(f32[128,128]{1,0:T(8,128)S(1)} %get-tuple-element.156), channel_id=1, source_target_pairs={{0,23},{1,22},{2,21},{3,20},{4,19},{5,18},{6,17},{7,16},{8,31},{9,... | collective-permute-start | bytes 196616 | tf_op jit(solution)/shard_map/ppermute | solution.py:429
  202.6 9.4 %collective-permute-start.55 = (f32[128,128]{1,0:T(8,128)S(1)}, f32[128,128]{1,0:T(8,128)S(1)}, u32[]{:S(2)}, u32[]{:S(2)}) collective-permute-start(f32[128,128]{1,0:T(8,128)S(1)} %get-tuple-element.158), channel_id=1, source_target_pairs={{0,25},{1,24},{2,27},{3,26},{4,29},{5,28},{6,31},{7,30},{8,17},{9,... | collective-permute-start | bytes 196616 | tf_op jit(solution)/shard_map/ppermute | solution.py:429
  204.9 17.3 %collective-permute-start.57 = (f32[128,128]{1,0:T(8,128)S(1)}, f32[128,128]{1,0:T(8,128)S(1)}, u32[]{:S(2)}, u32[]{:S(2)}) collective-permute-start(f32[128,128]{1,0:T(8,128)S(1)} %get-tuple-element.160), channel_id=1, source_target_pairs={{0,27},{1,26},{2,25},{3,24},{4,31},{5,30},{6,29},{7,28},{8,19},{9,... | collective-permute-start | bytes 196616 | tf_op jit(solution)/shard_map/ppermute | solution.py:429
  207.9 14.3 %collective-permute-start.58 = (f32[128,128]{1,0:T(8,128)S(1)}, f32[128,128]{1,0:T(8,128)S(1)}, u32[]{:S(2)}, u32[]{:S(2)}) collective-permute-start(f32[128,128]{1,0:T(8,128)S(1)} %get-tuple-element.161), channel_id=1, source_target_pairs={{0,28},{1,29},{2,30},{3,31},{4,24},{5,25},{6,26},{7,27},{8,20},{9,... | collective-permute-start | bytes 196616 | tf_op jit(solution)/shard_map/ppermute | solution.py:429
  209.3 12.9 %collective-permute-start.59 = (f32[128,128]{1,0:T(8,128)S(1)}, f32[128,128]{1,0:T(8,128)S(1)}, u32[]{:S(2)}, u32[]{:S(2)}) collective-permute-start(f32[128,128]{1,0:T(8,128)S(1)} %get-tuple-element.162), channel_id=1, source_target_pairs={{0,29},{1,28},{2,31},{3,30},{4,25},{5,24},{6,27},{7,26},{8,21},{9,... | collective-permute-start | bytes 196616 | tf_op jit(solution)/shard_map/ppermute | solution.py:429
  212.0 10.2 %collective-permute-start.60 = (f32[128,128]{1,0:T(8,128)S(1)}, f32[128,128]{1,0:T(8,128)S(1)}, u32[]{:S(2)}, u32[]{:S(2)}) collective-permute-start(f32[128,128]{1,0:T(8,128)S(1)} %get-tuple-element.163), channel_id=1, source_target_pairs={{0,30},{1,31},{2,28},{3,29},{4,26},{5,27},{6,24},{7,25},{8,22},{9,... | collective-permute-start | bytes 196616 | tf_op jit(solution)/shard_map/ppermute | solution.py:429
  212.6 9.7 %collective-permute-start.61 = (f32[128,128]{1,0:T(8,128)S(1)}, f32[128,128]{1,0:T(8,128)S(1)}, u32[]{:S(2)}, u32[]{:S(2)}) collective-permute-start(f32[128,128]{1,0:T(8,128)S(1)} %get-tuple-element.164), channel_id=1, source_target_pairs={{0,31},{1,30},{2,29},{3,28},{4,27},{5,26},{6,25},{7,24},{8,23},{9,... | collective-permute-start | bytes 196616 | tf_op jit(solution)/shard_map/ppermute | solution.py:429
  (38 other events, 722.8 us)
where the time goes:
time: 237 us
  starting transfers between devices  156 us (66%)
  waiting for transfers between devices  45.5 us (19%)
  Pallas kernels  31 us (13%)
  local copies, waits for them, and re-layouts  2.8 us (1%)
    ppermute x93, starting transfers between devices, exchange(): arrived[m] = lax.ppermute(blocks[m], ('gx', 'gy'), moves)  156 us
    ppermute x93, waiting for transfers between devices, exchange(): arrived[m] = lax.ppermute(blocks[m], ('gx', 'gy'), moves)  45.5 us
    pallas_call x2, Pallas kernels, x_waves(): pl.pallas_call(functools.partial(x_kernel, devices, x_local, y_local, ind...  11.1 us
    pallas_call x1, Pallas kernels, last_waves(): pl.pallas_call(functools.partial(last_kernel, devices, x_local, y_local,...  8.56 us
    pallas_call x2, Pallas kernels, slab_waves(): pl.pallas_call(functools.partial(slab_kernel, comps, x_local, blocks, per...  8.46 us
  transfers between devices with their start and end apart: 93, of which 13 were waited for; matrix products, arithmetic and copies ran while one was open for 0% of the time, Pallas kernels for 5%

commit v1 on v0

--- a/solution.py
+++ b/solution.py
@@ -92,84 +92,97 @@
     return (real * cos_k + imag * sin_k, imag * cos_k - real * sin_k)
 
 
-def pack_kernel(devices, per_owner, count, me, owner_row, slot_row, tiles, *out):
+def pack_kernel(
+    devices, per_owner, comps, with_slots, count, me, owner_row, slot_row, tiles, *refs
+):
+    out, held, sems = refs[-3:]
     listed = owner_row.shape[1]
-    comps = tiles.shape[1]
+    fetches = [
+        pltpu.make_async_copy(tiles.at[:, comp], held.at[i], sems.at[i])
+        for i, comp in enumerate(comps)
+    ]
+    for fetch in fetches:
+        fetch.start()
     live_count = count[0]
     owners = owner_row[...]
     live = lax.broadcasted_iota(jnp.int32, (1, listed), 1) < live_count
-    place = jnp.where(live, owners ^ me[0], -1)
-    named = jnp.where(
-        lax.broadcasted_iota(jnp.int32, (devices, listed), 0) == place, 1.0, 0.0
-    )
+    owner_at = lax.broadcasted_iota(jnp.int32, (devices, listed), 0)
+    named = jnp.where((owner_at == owners) & live, 1.0, 0.0)
     sender = lax.broadcasted_iota(jnp.int32, (listed, listed), 0)
     reader = lax.broadcasted_iota(jnp.int32, (listed, listed), 1)
     before = jnp.where(sender < reader, 1.0, 0.0).astype(jnp.bfloat16)
     counted = jnp.dot(named.astype(jnp.bfloat16), before, preferred_element_type=jnp.float32)
     rank = jnp.sum(counted * named, axis=0, keepdims=True).astype(jnp.int32)
-    target = jnp.where(live, place * per_owner + rank, -1)
+    target = jnp.where(live, owners * per_owner + rank, -1)
     places = lax.broadcasted_iota(jnp.int32, (devices * per_owner, listed), 0)
     chosen = jnp.where(places == target, 1.0, 0.0).astype(jnp.bfloat16)
-    for comp in range(comps):
-        parts = [part for r in range(2) for part in split_three(tiles[r, comp])]
+    if with_slots:
+        stated = slot_row[...] + 1
+        lane = rank + (me[0] & (128 // per_owner - 1)) * per_owner
+        lane_at = lax.broadcasted_iota(jnp.int32, (128, listed), 0)
+        ranked = jnp.where(lane_at == lane, 1.0, 0.0).astype(jnp.bfloat16)
+        coarse = (named * (stated >> 5).astype(jnp.float32)).astype(jnp.bfloat16)
+        fine = (named * (stated & 31).astype(jnp.float32)).astype(jnp.bfloat16)
+        slots = 32.0 * dot_rows(coarse, ranked) + dot_rows(fine, ranked)
+        out[:, 2 * len(comps) * per_owner :, :] = jnp.broadcast_to(
+            slots[:, None, :], (devices, 8, 128)
+        )
+    for i, fetch in enumerate(fetches):
+        fetch.wait()
+        parts = [part for r in range(2) for part in split_three(held[i, r])]
         got = jnp.dot(
             chosen, jnp.concatenate(parts, axis=1), preferred_element_type=jnp.float32
         )
         for r in range(2):
             one = got[:, 384 * r : 384 * r + 384]
             whole = (one[:, :128] + one[:, 128:256]) + one[:, 256:]
-            start = (2 * comp + r) * per_owner
-            for part in range(devices):
-                out[part][start : start + per_owner, :] = whole[part * per_owner :][:per_owner]
-    stated = slot_row[...] + 1
-    lane = rank + (place & (128 // per_owner - 1)) * per_owner
-    lane_at = lax.broadcasted_iota(jnp.int32, (128, listed), 0)
-    ranked = jnp.where(lane_at == lane, 1.0, 0.0).astype(jnp.bfloat16)
-    coarse = (named * (stated >> 5).astype(jnp.float32)).astype(jnp.bfloat16)
-    fine = (named * (stated & 31).astype(jnp.float32)).astype(jnp.bfloat16)
-    slots = 32.0 * dot_rows(coarse, ranked) + dot_rows(fine, ranked)
-    for part in range(devices):
-        out[part][2 * comps * per_owner :, :] = jnp.broadcast_to(slots[part : part + 1], (8, 128))
-
-
-def pack(tiles, owner_row, slot_row, count, me, devices, per_owner):
-    comps, listed = tiles.shape[1:3]
-    rows = 2 * comps * per_owner + 8
+            start = (2 * i + r) * per_owner
+            out[:, start : start + per_owner, :] = whole.reshape(devices, per_owner, 128)
+
+
+def pack(tiles, comps, owner_row, slot_row, count, me, after, devices, per_owner):
+    listed = tiles.shape[2]
+    with_slots = after is None
+    rows = 2 * len(comps) * per_owner + (8 if with_slots else 0)
+    extra = () if with_slots else (after,)
     return pl.pallas_call(
-        functools.partial(pack_kernel, devices, per_owner),
-        out_shape=[jax.ShapeDtypeStruct((rows, 128), jnp.float32)] * devices,
+        functools.partial(pack_kernel, devices, per_owner, comps, with_slots),
+        out_shape=jax.ShapeDtypeStruct((devices, rows, 128), jnp.float32),
         in_specs=[pl.BlockSpec(memory_space=pltpu.SMEM)] * 2
-        + [pl.BlockSpec(memory_space=pltpu.VMEM)] * 3,
-        out_specs=[pl.BlockSpec(memory_space=pltpu.VMEM)] * devices,
+        + [pl.BlockSpec(memory_space=pltpu.VMEM)] * 2
+        + [pl.BlockSpec(memory_space=pl.ANY)] * (1 + len(extra)),
+        out_specs=pl.BlockSpec(memory_space=pltpu.VMEM),
+        scratch_shapes=[
+            pltpu.VMEM((len(comps), 2, listed, 128), jnp.float32),
+            pltpu.SemaphoreType.DMA((len(comps),)),
+        ],
         compiler_params=params(24),
         cost_estimate=cost(
-            devices * per_owner * listed * 768 * 2 * comps, devices * rows * 1024
+            devices * per_owner * listed * 768 * 2 * len(comps), devices * rows * 1024
         ),
-    )(count, me, owner_row, slot_row, tiles)
-
-
-def slab_kernel(comps, x_local, blocks, per_owner, me, table, twist, *refs):
-    devices, kept = table.shape[:2]
-    data, out = refs[:devices], refs[devices : 2 * devices]
-    slab, turned, ordered = refs[2 * devices :]
+    )(count, me, owner_row, slot_row, tiles, *extra)
+
+
+def slab_kernel(
+    comps, places, x_local, blocks, per_owner, slots, table, twist, data, out, slab, turned
+):
+    devices = data.shape[0]
     entries = devices * per_owner
-    y_local = kept * blocks
+    y_local = blocks * 128 // devices
     wide = 2 * x_local
     shift = blocks.bit_length() - 1
     every = 128 // per_owner
-    slots = []
-    for start in range(0, devices, every):
-        slots.append(sum([one[one.shape[0] - 8 :, :][:1] for one in data[start : start + every]]))
-    slot = jnp.concatenate(slots, axis=1).astype(jnp.int32) - 1
+    stated = [
+        sum([slots[o, :1] for o in range(start, start + every)])
+        for start in range(0, devices, every)
+    ]
+    slot = jnp.concatenate(stated, axis=1).astype(jnp.int32) - 1
     landing = jnp.where(slot >= 0, (slot & (blocks - 1)) * x_local + (slot >> shift), -1)
-    for place in range(devices):
-        ordered[place * kept : (place + 1) * kept, :] = table[me[0] ^ place]
     for index, comp in enumerate(comps):
         parts = []
         for r in range(2):
-            start = (2 * comp + r) * per_owner
-            arrived = jnp.concatenate([one[start : start + per_owner, :] for one in data])
-            parts.extend(split_two(arrived))
+            start = (2 * places[index] + r) * per_owner
+            parts.extend(split_two(data[:, start : start + per_owner, :].reshape(entries, 128)))
         parts = jnp.concatenate(parts, axis=1)
         for start in range(0, blocks * x_local, 256):
             place = start + lax.broadcasted_iota(jnp.int32, (256, entries), 0)
@@ -203,42 +216,44 @@
         together = 4
         for start in range(0, blocks, together):
             moved = dot_rows_split(
-                ordered[...], turned[start * wide : (start + together) * wide, :]
+                table[...], turned[start * wide : (start + together) * wide, :]
             )
             for k in range(start, start + together):
                 one = moved[:, (k - start) * wide : (k - start + 1) * wide]
-                for part in range(devices):
-                    rows = pl.ds(index * y_local + k, kept, stride=blocks)
-                    out[part][rows, :] = one[part * kept : (part + 1) * kept]
-
-
-def slab_waves(me, comps, data, x_local, blocks, per_owner):
-    devices = len(data)
+                if len(comps) == 1:
+                    out[pl.ds(k, 128, stride=blocks), :] = one
+                else:
+                    kept = 128 // devices
+                    for o in range(devices):
+                        rows = pl.ds((o * len(comps) + index) * y_local + k, kept, stride=blocks)
+                        out[rows, :] = one[o * kept : (o + 1) * kept]
+
+
+def slab_waves(slots, comps, places, data, x_local, blocks, per_owner):
+    devices = data.shape[0]
     y_cells = blocks * 128
     fine = angles(128, 128, 128)
     table = np.concatenate([np.cos(fine), np.sin(fine)], axis=1).astype(np.float32)
-    table = table.reshape(devices, 128 // devices, 256)
     twist_angle = angles(blocks, 128, y_cells)
     twist = np.stack([np.cos(twist_angle), np.sin(twist_angle)]).astype(np.float32)
     entries = devices * per_owner
-    made = jax.ShapeDtypeStruct((len(comps) * y_cells // devices, 2 * x_local), jnp.float32)
-    return pl.pallas_call(
-        functools.partial(slab_kernel, comps, x_local, blocks, per_owner),
-        out_shape=[made] * devices,
-        in_specs=[pl.BlockSpec(memory_space=pltpu.SMEM)]
-        + [pl.BlockSpec(memory_space=pltpu.VMEM)] * (2 + devices),
-        out_specs=[pl.BlockSpec(memory_space=pltpu.VMEM)] * devices,
+    rows = len(comps) * y_cells
+    made = pl.pallas_call(
+        functools.partial(slab_kernel, comps, places, x_local, blocks, per_owner),
+        out_shape=jax.ShapeDtypeStruct((rows, 2 * x_local), jnp.float32),
+        in_specs=[pl.BlockSpec(memory_space=pltpu.VMEM)] * 4,
+        out_specs=pl.BlockSpec(memory_space=pltpu.VMEM),
         scratch_shapes=[
             pltpu.VMEM((2, blocks * x_local, 128), jnp.float32),
             pltpu.VMEM((blocks * 2 * x_local, 256), jnp.float32),
-            pltpu.VMEM((128, 256), jnp.float32),
         ],
         compiler_params=params(24),
         cost_estimate=cost(
             len(comps) * (blocks * x_local * entries * 1024 + y_cells * x_local * 3072),
             len(comps) * (entries * 1024 + y_cells * x_local * 8),
         ),
-    )(me, jnp.asarray(table), jnp.asarray(twist), *data)
+    )(slots, jnp.asarray(table), jnp.asarray(twist), data)
+    return made.reshape(devices, rows // devices, 2 * x_local)
 
 
 def swap_parts(value, x_local):
@@ -248,13 +263,11 @@
 
 
 def x_steps(
-    devices, x_local, y_local, index, me, twist, table, data, placed, turned, columns, store
+    devices, x_local, y_local, index, twist, table, data, turned, columns, store
 ):
     wide = 2 * x_local
     lane = lax.broadcasted_iota(jnp.int32, (1, wide), 1)
     sign = jnp.where(lane < x_local, 1.0, -1.0)
-    for place in range(devices):
-        placed[me[0] ^ place] = data[place][index * y_local : (index + 1) * y_local, :]
 
     def times(value, k, length):
         if k == 0:
@@ -269,7 +282,7 @@
     @pl.loop(0, y_local // 8)
     def _(step):
         at = pl.multiple_of(step * 8, 8)
-        values = [placed[o, pl.ds(at, 8), :] for o in range(devices)]
+        values = [data[o, pl.ds(index * y_local + at, 8), :] for o in range(devices)]
         waves = flat_fft(values, times)
         for k in range(devices):
             swapped = swap_parts(waves[k], x_local)
@@ -289,19 +302,19 @@
         store(start, columns[start : start + 128, :].T)
 
 
-def x_kernel(devices, x_local, y_local, index, me, twist, table, *refs):
-    data, out, scratch = refs[:devices], refs[devices], refs[devices + 1 :]
+def x_kernel(devices, x_local, y_local, index, twist, table, data, *refs):
+    out, scratch = refs[0], refs[1:]
 
     def store(start, block):
         out[0, :, start : start + 128] = block[:y_local]
         out[1, :, start : start + 128] = block[y_local:]
 
-    x_steps(devices, x_local, y_local, index, me, twist, table, data, *scratch, store)
-
-
-def last_kernel(devices, x_local, y_local, index, me, twist, table, *refs):
-    data, (green, first, second, out) = refs[:devices], refs[devices : devices + 4]
-    scratch, (tensor, kept, made, in_sems, out_sems) = refs[devices + 4 :][:3], refs[devices + 7 :]
+    x_steps(devices, x_local, y_local, index, twist, table, data, *scratch, store)
+
+
+def last_kernel(devices, x_local, y_local, index, twist, table, data, *refs):
+    green, first, second, out = refs[:4]
+    scratch, (tensor, kept, made, in_sems, out_sems) = refs[4:6], refs[6:]
     x_cells = devices * x_local
     pieces = made.shape[0]
     width = x_cells // pieces
@@ -317,7 +330,7 @@
         kept[2, 0, :, start : start + 128] = block[:y_local]
         kept[2, 1, :, start : start + 128] = block[y_local:]
 
-    x_steps(devices, x_local, y_local, index, me, twist, table, data, *scratch, store)
+    x_steps(devices, x_local, y_local, index, twist, table, data, *scratch, store)
     for fetch in fetches:
         fetch.wait()
     sends = []
@@ -374,34 +387,31 @@
 
 def x_scratch(devices, x_local, y_local):
     return [
-        pltpu.VMEM((devices, y_local, 2 * x_local), jnp.float32),
         pltpu.VMEM((devices, 2 * y_local, 2 * x_local), jnp.float32),
         pltpu.VMEM((devices * x_local, 2 * y_local), jnp.float32),
     ]
 
 
-def x_waves(me, index, data, devices, x_local, y_local, y_cells):
+def x_waves(index, data, devices, x_local, y_local, y_cells):
     x_cells = devices * x_local
     return pl.pallas_call(
         functools.partial(x_kernel, devices, x_local, y_local, index),
         out_shape=jax.ShapeDtypeStruct((2, y_local, x_cells), jnp.float32),
-        in_specs=[pl.BlockSpec(memory_space=pltpu.SMEM)]
-        + [pl.BlockSpec(memory_space=pltpu.VMEM)] * (2 + devices),
+        in_specs=[pl.BlockSpec(memory_space=pltpu.VMEM)] * 3,
         out_specs=pl.BlockSpec(memory_space=pltpu.VMEM),
         scratch_shapes=x_scratch(devices, x_local, y_local),
         compiler_params=params(24),
         cost_estimate=cost(x_cells * y_local * x_local * 24, x_cells * y_local * 16),
-    )(me, *x_tables(devices, x_local, y_cells), *data)
-
-
-def last_waves(me, index, data, green, first, second, devices, x_local, y_local, y_cells):
+    )(*x_tables(devices, x_local, y_cells), data)
+
+
+def last_waves(index, data, green, first, second, devices, x_local, y_local, y_cells):
     x_cells = devices * x_local
     pieces = 8
     return pl.pallas_call(
         functools.partial(last_kernel, devices, x_local, y_local, index),
         out_shape=jax.ShapeDtypeStruct((2, 3, y_local, x_cells), jnp.float32),
-        in_specs=[pl.BlockSpec(memory_space=pltpu.SMEM)]
-        + [pl.BlockSpec(memory_space=pltpu.VMEM)] * (2 + devices)
+        in_specs=[pl.BlockSpec(memory_space=pltpu.VMEM)] * 3
         + [pl.BlockSpec(memory_space=pl.ANY)] * 3,
         out_specs=pl.BlockSpec(memory_space=pl.ANY),
         scratch_shapes=x_scratch(devices, x_local, y_local)
@@ -414,20 +424,27 @@
         ],
         compiler_params=params(40),
         cost_estimate=cost(x_cells * y_local * (x_local * 24 + 72), x_cells * y_local * 96),
-    )(me, *x_tables(devices, x_local, y_cells), *data, green, first, second)
-
-
-def exchange(blocks):
-    devices = len(blocks)
-    far = [m for m in range(devices) if m & 4]
-    near = [m for m in range(1, devices) if not m & 4]
-    arrived = [blocks[0]] + [None] * (devices - 1)
-    for pair in zip(far, near + [None]):
-        for m in pair:
-            if m is not None:
-                moves = [(d, d ^ m) for d in range(devices)]
-                arrived[m] = lax.ppermute(blocks[m], ("gx", "gy"), moves)
-    return arrived
+    )(*x_tables(devices, x_local, y_cells), data, green, first, second)
+
+
+def gate_kernel(data, after, out):
+    del data, after, out
+
+
+def once_after(data, after):
+    return pl.pallas_call(
+        gate_kernel,
+        out_shape=jax.ShapeDtypeStruct(data.shape, data.dtype),
+        in_specs=[pl.BlockSpec(memory_space=pl.ANY)] * 2,
+        out_specs=pl.BlockSpec(memory_space=pl.ANY),
+        input_output_aliases={0: 0},
+        compiler_params=params(1),
+        cost_estimate=cost(0, 0),
+    )(data, after)
+
+
+def exchange(data):
+    return lax.all_to_all(data, ("gx", "gy"), split_axis=0, concat_axis=0, tiled=True)
 
 
 def per_device(tiles, tile_owner, tile_slot, tile_count, green):
@@ -439,18 +456,22 @@
     blocks = y_cells // tile_len
     per_owner = max(2, 2 * tile_total // devices)
     assert planes == 1 and tile_len == 128
-    me = (lax.axis_index("gx") * lax.axis_size("gy") + lax.axis_index("gy")).reshape(1)
-    me = me.astype(jnp.int32)
     owner_row, slot_row = tile_owner.reshape(1, tile_total), tile_slot.reshape(1, tile_total)
     green = green.reshape(2, 6, y_local, x_cells)
-    arrived = exchange(pack(tiles, owner_row, slot_row, tile_count, me, devices, per_owner))
-    moved = {}
-    for comps in ((0,), (1, 2)):
-        got = exchange(slab_waves(me, comps, arrived, x_local, blocks, per_owner))
-        moved.update({comp: (me, i, got) for i, comp in enumerate(comps)})
+    me = (lax.axis_index("gx") * lax.axis_size("gy") + lax.axis_index("gy")).reshape(1)
+    lists = (owner_row, slot_row, tile_count, me.astype(jnp.int32))
+    early = pack(tiles, (0, 1), *lists, None, devices, per_owner)
+    late = pack(tiles, (2,), *lists, early, devices, per_owner)
+    early, late = exchange(early), exchange(late)
+    slots = early[:, 4 * per_owner :, :]
+    grid = (x_local, blocks, per_owner)
+    early = slab_waves(slots, (0, 1), (0, 1), early, *grid)
+    early = exchange(once_after(early, late))
+    late = slab_waves(slots, (2,), (0,), late, *grid)
+    late = exchange(once_after(late, early))
     sizes = (devices, x_local, y_local, y_cells)
-    waves = [x_waves(*moved[comp], *sizes) for comp in range(2)]
-    mixed = last_waves(*moved[2], green, *waves, *sizes)
+    waves = [x_waves(comp, early, *sizes) for comp in range(2)]
+    mixed = last_waves(0, late, green, *waves, *sizes)
     return mixed.reshape(2, 3, planes, y_local, x_cells)
 
 

time: 237 us -> 202 us (0.85)
  starting transfers between devices: 156 us -> 16.9 us
  waiting for transfers between devices: 45.5 us -> 131 us
  local copies, waits for them, and re-layouts: 2.8 us -> 17.6 us
  Pallas kernels: 31 us -> 35.5 us
    ppermute x93 -> x0, starting transfers between devices: 156 us -> none  [exchange(): arrived[m] = lax.ppermute(blocks[m], ('gx', 'gy'), moves)]
    all_to_all x0 -> x4, waiting for transfers between devices: none -> 131 us  [exchange(): lax.all_to_all(data, ('gx', 'gy'), split_axis=0, concat_axis=0, tiled=True)]
    ppermute x93 -> x0, waiting for transfers between devices: 45.5 us -> none  [exchange(): arrived[m] = lax.ppermute(blocks[m], ('gx', 'gy'), moves)]
    all_to_all x0 -> x4, starting transfers between devices: none -> 16.9 us  [exchange(): lax.all_to_all(data, ('gx', 'gy'), split_axis=0, concat_axis=0, tiled=True)]
    unnamed x18 -> x38, local copies, waits for them, and re-layouts: 2.8 us -> 16.7 us
    pallas_call x3 -> x6, Pallas kernels: 11.4 us -> 15.3 us  [the longest x2 8.11 us: slab_waves(): pl.pallas_call(functools.partial(slab_kernel, comps, places, x_local, blo...]
  transfers between devices with their start and end apart: 93 -> 4, of which waited for: 13 -> 4; matrix products, arithmetic and copies ran while one was open for 0% -> 0% of each run, Pallas kernels for 5% -> 11%
where the time goes in v1:
time: 202 us
  waiting for transfers between devices  131 us (65%)
  Pallas kernels  35.5 us (18%)
  local copies, waits for them, and re-layouts  17.6 us (9%)
  starting transfers between devices  16.9 us (8%)
    all_to_all x4, waiting for transfers between devices, exchange(): lax.all_to_all(data, ('gx', 'gy'), split_axis=0, concat_axis=0, tiled=True)  131 us
    all_to_all x4, starting transfers between devices, exchange(): lax.all_to_all(data, ('gx', 'gy'), split_axis=0, concat_axis=0, tiled=True)  16.9 us
    unnamed x38, local copies, waits for them, and re-layouts  16.7 us
    pallas_call x2, Pallas kernels, x_waves(): pl.pallas_call(functools.partial(x_kernel, devices, x_local, y_local, ind...  10.7 us
    pallas_call x1, Pallas kernels, last_waves(): pl.pallas_call(functools.partial(last_kernel, devices, x_local, y_local,...  9.64 us
    pallas_call x2, Pallas kernels, slab_waves(): pl.pallas_call(functools.partial(slab_kernel, comps, places, x_local, blo...  8.11 us
    pallas_call x2, Pallas kernels, pack(): pl.pallas_call(functools.partial(pack_kernel, devices, per_owner, comps,...  7.15 us
  transfers between devices with their start and end apart: 4, of which 4 were waited for; matrix products, arithmetic and copies ran while one was open for 0% of the time, Pallas kernels for 11%

profile of v1, /device:TPU:0, one launch (start us, length us, event | category | flops | bytes accessed | tf_op | source)
XLA Modules:
  0.0 201.7 jit_solution(16123733586977011097)
XLA Ops:
  0.7 0.0 copy-start.9
  0.7 1.4 copy-done.9
  2.1 0.0 copy-start.13
  2.1 0.7 copy-done.13
  2.7 0.0 copy-start.15
  2.8 0.7 copy-done.15
  3.4 4.6 %shard_map.145.refs_0_ = f32[32,136,128]{2,1,0:T(8,128)} custom-call(s32[1]{0:T(128)S(6)} %copy.21.count, s32[1]{0:T(128)} %bitcast.me, s32[1,512]{1,0:T(1,128)S(1)} %bitcast.12, s32[1,512]{1,0:T(1,128)S(1)} %bitcast.14, f32[2,3,512,128]{3,2,1,0:T(8,128)S(1)} %copy-done.9), custom_call_target="tpu_custom_call" | custom-call | flops 1610612736 | bytes 4456448 | tf_op jit(solution)/shard_map/pallas_call | solution.py:148
  8.1 0.0 copy-start.14
  8.1 0.0 copy-start.16
  8.1 7.3 %all-to-all-start = ((f32[32,136,128]{2,1,0:T(8,128)}), f32[32,136,128]{2,1,0:T(8,128)S(1)}, u32[]{:S(2)}, u32[]{:S(2)}) async-start(f32[32,136,128]{2,1,0:T(8,128)} %shard_map.145.refs_0_), calls=%async_computation | async-start | bytes 4456448 | tf_op jit(solution)/shard_map/all_to_all | solution.py:447
  15.4 0.0 copy-done.14
  15.4 0.0 copy-done.16
  15.4 0.0 copy-start.10
  15.4 1.4 copy-done.10
  16.8 2.5 %shard_map.146 = f32[32,64,128]{2,1,0:T(8,128)} custom-call(s32[1]{0:T(128)S(6)} %copy.21.count, s32[1]{0:T(128)} %bitcast.me, s32[1,512]{1,0:T(1,128)S(1)} %bitcast.13, s32[1,512]{1,0:T(1,128)S(1)} %bitcast.15, f32[2,3,512,128]{3,2,1,0:T(8,128)S(1)} %copy-done.10, f32[32,136,128]{2,1,0:T(8,128)} %shard_map.145.refs_0_), custom_call_target="tpu_custom_call" | custom-call | flops 805306368 | bytes 2097152 | tf_op jit(solution)/shard_map/pallas_call | solution.py:148
  19.4 0.0 copy-start.17
  19.4 0.0 copy-start.18
  19.4 48.9 %all-to-all-done.data = f32[32,136,128]{2,1,0:T(8,128)S(1)} async-done(((f32[32,136,128]{2,1,0:T(8,128)}), f32[32,136,128]{2,1,0:T(8,128)S(1)}, u32[]{:S(2)}, u32[]{:S(2)}) %all-to-all-start) | async-done | bytes 2228256 | tf_op jit(solution)/shard_map/all_to_all | solution.py:447
  68.3 0.0 copy-start.7
  68.3 1.4 copy-done.7
  69.7 3.3 %all-to-all-start.1 = ((f32[32,64,128]{2,1,0:T(8,128)}), f32[32,64,128]{2,1,0:T(8,128)S(1)}, u32[]{:S(2)}, u32[]{:S(2)}) async-start(f32[32,64,128]{2,1,0:T(8,128)} %shard_map.146), calls=%async_computation.1 | async-start | bytes 2097152 | tf_op jit(solution)/shard_map/all_to_all | solution.py:447
  73.0 0.9 slice.4.slots
  73.9 0.0 copy-done.17
  73.9 0.0 copy-done.18
  74.0 0.0 copy-start.8
  74.0 1.6 copy-done.8
  75.6 5.4 %shard_map.148 = f32[4096,128]{1,0:T(8,128)S(1)} custom-call(f32[32,8,128]{2,1,0:T(8,128)S(1)} %slice.4.slots, f32[128,256]{1,0:T(8,128)S(1)} %copy-done.17, f32[2,16,128]{2,1,0:T(8,128)S(1)} %copy-done.18, f32[32,136,128]{2,1,0:T(8,128)S(1)} %copy-done.8), custom_call_target="tpu_custom_call" | custom-call | flops 2952790016 | bytes 4194304 | tf_op jit(solution)/shard_map/pallas_call | solution.py:241
  81.0 19.6 %all-to-all-done.1.data.after = f32[32,64,128]{2,1,0:T(8,128)S(1)} async-done(((f32[32,64,128]{2,1,0:T(8,128)}), f32[32,64,128]{2,1,0:T(8,128)S(1)}, u32[]{:S(2)}, u32[]{:S(2)}) %all-to-all-start.1) | async-done | bytes 1048608 | tf_op jit(solution)/shard_map/all_to_all | solution.py:447
  100.6 0.0 copy-start
  100.6 1.3 copy-done
  101.9 2.7 %all-to-all-start.2 = ((f32[32,128,128]{2,1,0:T(8,128)}), f32[32,128,128]{2,1,0:T(8,128)S(1)}, u32[]{:S(2)}, u32[]{:S(2)}) async-start(f32[32,128,128]{2,1,0:T(8,128)} %copy-done), calls=%async_computation.2 | async-start | bytes 4194304 | tf_op jit(solution)/shard_map/all_to_all | solution.py:447
  104.7 2.7 %shard_map.147 = f32[2048,128]{1,0:T(8,128)S(1)} custom-call(f32[32,8,128]{2,1,0:T(8,128)S(1)} %slice.4.slots, f32[128,256]{1,0:T(8,128)S(1)} %copy-done.17, f32[2,16,128]{2,1,0:T(8,128)S(1)} %copy-done.18, f32[32,64,128]{2,1,0:T(8,128)S(1)} %all-to-all-done.1.data.after), custom_call_target="tpu_custom_call" | custom-call | flops 1476395008 | bytes 2097152 | tf_op jit(solution)/shard_map/pallas_call | solution.py:241
  107.4 0.0 copy-start.4
  107.4 1.0 copy-done.4
  108.4 46.3 %all-to-all-done.2.after.data = f32[32,128,128]{2,1,0:T(8,128)S(1)} async-done(((f32[32,128,128]{2,1,0:T(8,128)}), f32[32,128,128]{2,1,0:T(8,128)S(1)}, u32[]{:S(2)}, u32[]{:S(2)}) %all-to-all-start.2) | async-done | bytes 2097184 | tf_op jit(solution)/shard_map/all_to_all | solution.py:447
  154.7 0.0 copy-start.5
  154.7 1.2 copy-done.5
  155.9 0.0 copy-start.11
  155.9 0.0 copy-start.12
  156.0 0.0 copy-start.6
  156.0 1.0 copy-done.6
  156.9 3.6 %all-to-all-start.3 = ((f32[32,64,128]{2,1,0:T(8,128)}), f32[32,64,128]{2,1,0:T(8,128)}, u32[]{:S(2)}, u32[]{:S(2)}) async-start(f32[32,64,128]{2,1,0:T(8,128)} %copy-done.6), calls=%async_computation.3 | async-start | bytes 2097152 | tf_op jit(solution)/shard_map/all_to_all | solution.py:447
  160.5 0.0 copy-done.11
  160.5 0.0 copy-done.12
  160.5 5.3 %shard_map.151.refs_1_ = f32[2,64,2048]{2,1,0:T(8,128)S(1)} custom-call(f32[2,32,128]{2,1,0:T(8,128)S(1)} %copy-done.11, f32[64,128]{1,0:T(8,128)S(1)} %copy-done.12, f32[32,128,128]{2,1,0:T(8,128)S(1)} %all-to-all-done.2.after.data), custom_call_target="tpu_custom_call" | custom-call | flops 201326592 | bytes 2097152 | tf_op jit(solution)/shard_map/pallas_call | solution.py:397
  165.9 5.3 %shard_map.152.refs_2_ = f32[2,64,2048]{2,1,0:T(8,128)S(1)} custom-call(f32[2,32,128]{2,1,0:T(8,128)S(1)} %copy-done.11, f32[64,128]{1,0:T(8,128)S(1)} %copy-done.12, f32[32,128,128]{2,1,0:T(8,128)S(1)} %all-to-all-done.2.after.data), custom_call_target="tpu_custom_call" | custom-call | flops 201326592 | bytes 2097152 | tf_op jit(solution)/shard_map/pallas_call | solution.py:397
  171.2 0.0 copy-start.2
  171.2 1.0 copy-done.2
  172.2 15.7 %all-to-all-done.3.data = f32[32,64,128]{2,1,0:T(8,128)} async-done(((f32[32,64,128]{2,1,0:T(8,128)}), f32[32,64,128]{2,1,0:T(8,128)}, u32[]{:S(2)}, u32[]{:S(2)}) %all-to-all-start.3) | async-done | bytes 1048608 | tf_op jit(solution)/shard_map/all_to_all | solution.py:447
  187.9 0.0 copy-start.1
  187.9 2.8 %copy-done.1 = f32[2,6,1,64,2048]{4,3,2,1,0:T(8,128)S(1)} copy-done((f32[2,6,1,64,2048]{4,3,2,1,0:T(8,128)S(1)}, f32[2,6,1,64,2048]{4,3,2,1,0:T(8,128)}, u32[]{:S(2)}) %copy-start.1) | copy-done | bytes 6291480
  190.7 0.0 copy-start.3
  190.7 1.2 copy-done.3
  191.9 9.6 %shard_map.153 = f32[2,3,64,2048]{3,2,1,0:T(8,128)} custom-call(f32[2,32,128]{2,1,0:T(8,128)S(1)} %copy-done.11, f32[64,128]{1,0:T(8,128)S(1)} %copy-done.12, f32[32,64,128]{2,1,0:T(8,128)} %all-to-all-done.3.data, f32[2,6,64,2048]{3,2,1,0:T(8,128)S(1)} %bitcast.10, f32[2,64,2048]{2,1,0:T(8,128)S(1)} %shard_map.151.refs_1_, f32[2,64,2048]{2,1,0:T(8,128)S(1)} %copy-done.3), custom_call_target="tpu_custom_call" | custom-call | flops 210763776 | bytes 12582912 | tf_op jit(solution)/shard_map/pallas_call | solution.py:411
  (2 shorter events, 0.0 us)
Async XLA Ops:
  0.7 1.4 copy-start.9
  2.1 0.7 copy-start.13
  2.7 0.7 copy-start.15
  8.1 7.3 %copy-start.14 = (s32[512,1]{0,1:T(1,128)S(1)}, s32[512,1]{0,1:T(1,128)}, u32[]{:S(2)}) copy-start(s32[512,1]{0,1:T(1,128)} %param.16) | copy-start | bytes 6148
  8.1 7.3 %copy-start.16 = (s32[512]{0:T(512)S(1)}, s32[512]{0:T(512)}, u32[]{:S(2)}) copy-start(s32[512]{0:T(512)} %param.17) | copy-start | bytes 6148
  8.1 60.2 %all-to-all-start = ((f32[32,136,128]{2,1,0:T(8,128)}), f32[32,136,128]{2,1,0:T(8,128)S(1)}, u32[]{:S(2)}, u32[]{:S(2)}) async-start(f32[32,136,128]{2,1,0:T(8,128)} %shard_map.145.refs_0_), calls=%async_computation | async-start | bytes 4456448 | tf_op jit(solution)/shard_map/all_to_all | solution.py:447
  15.4 1.4 copy-start.10
  19.4 54.6 %copy-start.17 = (f32[128,256]{1,0:T(8,128)S(1)}, f32[128,256]{1,0:T(8,128)}, u32[]{:S(2)}) copy-start(f32[128,256]{1,0:T(8,128)} %constant.18.clone.table) | copy-start | bytes 393220
  19.4 54.6 %copy-start.18 = (f32[2,16,128]{2,1,0:T(8,128)S(1)}, f32[2,16,128]{2,1,0:T(8,128)}, u32[]{:S(2)}) copy-start(f32[2,16,128]{2,1,0:T(8,128)} %constant.19.clone.twist) | copy-start | bytes 49156
  68.3 1.4 copy-start.7
  69.7 30.9 %all-to-all-start.1 = ((f32[32,64,128]{2,1,0:T(8,128)}), f32[32,64,128]{2,1,0:T(8,128)S(1)}, u32[]{:S(2)}, u32[]{:S(2)}) async-start(f32[32,64,128]{2,1,0:T(8,128)} %shard_map.146), calls=%async_computation.1 | async-start | bytes 2097152 | tf_op jit(solution)/shard_map/all_to_all | solution.py:447
  74.0 1.6 copy-start.8
  100.6 1.3 copy-start
  101.9 52.8 %all-to-all-start.2 = ((f32[32,128,128]{2,1,0:T(8,128)}), f32[32,128,128]{2,1,0:T(8,128)S(1)}, u32[]{:S(2)}, u32[]{:S(2)}) async-start(f32[32,128,128]{2,1,0:T(8,128)} %copy-done), calls=%async_computation.2 | async-start | bytes 4194304 | tf_op jit(solution)/shard_map/all_to_all | solution.py:447
  107.4 1.0 copy-start.4
  154.7 1.2 copy-start.5
  155.9 4.6 %copy-start.11 = (f32[2,32,128]{2,1,0:T(8,128)S(1)}, f32[2,32,128]{2,1,0:T(8,128)}, u32[]{:S(2)}) copy-start(f32[2,32,128]{2,1,0:T(8,128)} %constant.20.clone.twist) | copy-start | bytes 98308
  155.9 4.6 %copy-start.12 = (f32[64,128]{1,0:T(8,128)S(1)}, f32[64,128]{1,0:T(8,128)}, u32[]{:S(2)}) copy-start(f32[64,128]{1,0:T(8,128)} %constant.21.clone.table) | copy-start | bytes 98308
  156.0 1.0 copy-start.6
  156.9 31.0 %all-to-all-start.3 = ((f32[32,64,128]{2,1,0:T(8,128)}), f32[32,64,128]{2,1,0:T(8,128)}, u32[]{:S(2)}, u32[]{:S(2)}) async-start(f32[32,64,128]{2,1,0:T(8,128)} %copy-done.6), calls=%async_computation.3 | async-start | bytes 2097152 | tf_op jit(solution)/shard_map/all_to_all | solution.py:447
  171.2 1.0 copy-start.2
  187.9 2.8 %copy-start.1 = (f32[2,6,1,64,2048]{4,3,2,1,0:T(8,128)S(1)}, f32[2,6,1,64,2048]{4,3,2,1,0:T(8,128)}, u32[]{:S(2)}) copy-start(f32[2,6,1,64,2048]{4,3,2,1,0:T(8,128)} %param.19) | copy-start | bytes 18874372
  190.7 1.2 copy-start.3
